TPU v7x, 512 devices: a whole 4x4x16 slice. The times are simulated.
512 devices in a mesh: seq: 64 (over z, y_hi, core), tp: 8 (over x, y_lo).
Axes of the slice: x: 4, y: 4 (y_hi: 2, y_lo: 2; y = y_hi * 2 + y_lo), z: 16, core: 2. Of those that a mesh axis runs over, the one named last changes fastest.
Arguments:
- q_proj: bfloat16 [8192, 8192], P('seq', 'tp'), may hold values from -6 to 6
- k_proj: bfloat16 [8192, 8192], P('seq', 'tp'), may hold values from -6 to 6
- v_proj: bfloat16 [8192, 8192], P('seq', 'tp'), may hold values from -6 to 6
- grad_out: bfloat16 [8192, 8192], P('seq', 'tp'), may hold values from -6 to 6
- w_first: float32 [32, 64], replicated, may hold values from -2 to 2
- w_second: float32 [64, 8192], P(None, 'tp'), may hold values from -0.75 to 0.75
- decay_rate: float32 [8192], P('tp'), may hold values from 0.02 to 256
- skip_gain: float32 [8192], P('tp'), may hold values from 0.5 to 1.5
Outputs:
- grad_q: bfloat16 [8192, 8192], P('seq', 'tp')
- grad_k: bfloat16 [8192, 8192], P('seq', 'tp')
- grad_v: bfloat16 [8192, 8192], P('seq', 'tp')
- grad_first: float32 [32, 64], replicated
- grad_second: float32 [64, 8192], P(None, 'tp')
- grad_decay: float32 [8192], P('tp')
- grad_skip: float32 [8192], P('tp')
All inputs are finite; a program needn't handle non-finite values.
Results may differ from a plain program's by a relative error of at most 0.0058.
Values may be sent and summed in bfloat16 or wider, within the bound.
A program may use at most 64 MiB of HBM per device.

v0:
```python
import math

import jax
import jax.numpy as jnp
from jax import lax
from jax.sharding import PartitionSpec as P

HIGH = lax.Precision.HIGHEST


def positional_table(length, band_count):
    positions = jnp.arange(length, dtype=jnp.int32)
    band_index = jnp.arange(band_count, dtype=jnp.int32)
    frequency = 3 * (band_index + 1) * (band_index + 1) + band_index
    phase_index = positions[:, None] * frequency[None, :] % length
    angles = phase_index.astype(jnp.float32) * (2.0 * math.pi / length)
    return jnp.concatenate([jnp.sin(angles), jnp.cos(angles)], axis=1)


def split_length(padded_len):
    size_one = 2
    divisor = 2
    while divisor * divisor <= padded_len:
        if padded_len % divisor == 0:
            size_one = divisor
        divisor = divisor + 2
    return (size_one, padded_len // size_one)


def square_tables(count, signed):
    indices = jnp.arange(count, dtype=jnp.int32)
    phase_index = indices[:, None] * indices[None, :] % count
    angles = phase_index.astype(jnp.float32) * (2.0 * math.pi / count)
    return (jnp.cos(angles), signed * jnp.sin(angles))


def block_table(count, signed):
    cos_part, sin_part = square_tables(count, signed)
    upper = jnp.concatenate([cos_part, sin_part], axis=1)
    lower = jnp.concatenate([-sin_part, cos_part], axis=1)
    return jnp.concatenate([upper, lower], axis=0)


def twiddle_tables(size_one, size_two, signed):
    padded_len = size_one * size_two
    rows_one = jnp.arange(size_one, dtype=jnp.int32)
    rows_two = jnp.arange(size_two, dtype=jnp.int32)
    phase_index = rows_one[:, None] * rows_two[None, :] % padded_len
    angles = phase_index.astype(jnp.float32) * (2.0 * math.pi / padded_len)
    return (jnp.cos(angles), signed * jnp.sin(angles))


def forward_dft(signal, size_one, size_two):
    batch_rows = signal.shape[0]
    half_one = size_one // 2
    shaped = signal.reshape(batch_rows, half_one, size_two)
    cos_one, sin_one = square_tables(size_one, -1.0)
    table_one = jnp.concatenate([cos_one[:, :half_one], sin_one[:, :half_one]], axis=0)
    section = jnp.einsum("ka,cab->ckb", table_one, shaped, precision=HIGH)
    part_real = section[:, :size_one]
    part_imag = section[:, size_one:]
    turn_real, turn_imag = twiddle_tables(size_one, size_two, -1.0)
    rotated = jnp.concatenate(
        [
            part_real * turn_real - part_imag * turn_imag,
            part_real * turn_imag + part_imag * turn_real,
        ],
        axis=2,
    )
    result = jnp.einsum("ckb,bm->ckm", rotated, block_table(size_two, -1.0), precision=HIGH)
    return (result[:, :, :size_two], result[:, :, size_two:])


def inverse_dft(spec_real, spec_imag, size_one, size_two):
    batch_rows = spec_real.shape[0]
    half_one = size_one // 2
    joined = jnp.concatenate([spec_real, spec_imag], axis=2)
    middle = jnp.einsum("ckm,mb->ckb", joined, block_table(size_two, 1.0), precision=HIGH)
    mid_real = middle[:, :, :size_two]
    mid_imag = middle[:, :, size_two:]
    turn_real, turn_imag = twiddle_tables(size_one, size_two, 1.0)
    rotated = jnp.concatenate(
        [mid_real * turn_real - mid_imag * turn_imag, mid_real * turn_imag + mid_imag * turn_real],
        axis=1,
    )
    cos_one, sin_one = square_tables(size_one, 1.0)
    table_one = jnp.concatenate([cos_one[:half_one], -sin_one[:half_one]], axis=1)
    result = jnp.einsum("ak,ckb->cab", table_one, rotated, precision=HIGH)
    return result.reshape(batch_rows, half_one * size_two) / float(size_one * size_two)


def times_spectrum(left, right, conjugate):
    left_real, left_imag = left
    right_real, right_imag = right
    if conjugate:
        left_imag = -left_imag
    return (
        left_real * right_real - left_imag * right_imag,
        left_real * right_imag + left_imag * right_real,
    )


def per_device(q_proj, k_proj, v_proj, grad_out, w_first, w_second, decay_rate, skip_gain):
    tok_rows, chan_tp = q_proj.shape
    seq_count = lax.axis_size("seq")
    length = tok_rows * seq_count
    chan_sub = chan_tp // seq_count
    seq_index = lax.axis_index("seq")
    scale_seq = length ** (-0.5)
    padded_len = 2 * length
    size_one, size_two = split_length(padded_len)
    gated_in = (k_proj.astype(jnp.float32) * v_proj.astype(jnp.float32)).astype(jnp.bfloat16)
    gated_grad = (grad_out.astype(jnp.float32) * q_proj.astype(jnp.float32)).astype(jnp.bfloat16)

    def to_channels(values):
        return values.T.reshape(seq_count, chan_sub, tok_rows)

    def to_rows(values):
        return values.reshape(chan_tp, tok_rows).T

    positional = positional_table(length, w_first.shape[0] // 2)
    sine_input = jnp.dot(positional, w_first, precision=HIGH, preferred_element_type=jnp.float32)
    hidden = jnp.sin(sine_input)
    offset = seq_index * chan_sub
    w_mine = lax.dynamic_slice_in_dim(w_second, offset, chan_sub, 1)
    decay_mine = lax.dynamic_slice_in_dim(decay_rate, offset, chan_sub, 0)
    skip_mine = lax.dynamic_slice_in_dim(skip_gain, offset, chan_sub, 0)
    fraction = jnp.arange(length).astype(jnp.float32) / length
    raw_filter = jnp.einsum("lf,fb->bl", hidden, w_mine, precision=HIGH)
    envelope = jnp.exp(-decay_mine[:, None] * fraction[None, :])
    long_filter = raw_filter * envelope * scale_seq
    spectrum_filter = forward_dft(long_filter, size_one, size_two)
    gated_block = lax.all_to_all(
        to_channels(gated_in), "seq", split_axis=0, concat_axis=2, tiled=True
    )
    gated_full = gated_block[0].astype(jnp.float32)
    spectrum_in = forward_dft(gated_full, size_one, size_two)
    conv_real, conv_imag = times_spectrum(spectrum_filter, spectrum_in, False)
    convolved = inverse_dft(conv_real, conv_imag, size_one, size_two)
    convolved = convolved + skip_mine[:, None] * gated_full
    gated_full, spectrum_in, conv_block = (
        gated_full,
        spectrum_in,
        convolved.astype(jnp.bfloat16)[None],
    )
    conv_back = lax.all_to_all(conv_block, "seq", split_axis=2, concat_axis=0, tiled=True)
    grad_block = lax.all_to_all(
        to_channels(gated_grad), "seq", split_axis=0, concat_axis=2, tiled=True
    )
    grad_full = grad_block[0].astype(jnp.float32)
    spectrum_grad = forward_dft(grad_full, size_one, size_two)
    back_real, back_imag = times_spectrum(spectrum_filter, spectrum_grad, True)
    grad_gated = inverse_dft(back_real, back_imag, size_one, size_two)
    grad_gated = grad_gated + skip_mine[:, None] * grad_full
    corr_real, corr_imag = times_spectrum(spectrum_in, spectrum_grad, True)
    grad_filter = inverse_dft(corr_real, corr_imag, size_one, size_two)
    grad_full, back_block, grad_filter = (
        grad_full,
        grad_gated.astype(jnp.bfloat16)[None],
        grad_filter,
    )
    grad_back = lax.all_to_all(back_block, "seq", split_axis=2, concat_axis=0, tiled=True)
    grad_raw = grad_filter * envelope * scale_seq
    skip_part = jnp.sum(grad_full * gated_full, axis=1) * scale_seq
    decay_part = -jnp.sum(grad_raw * raw_filter * fraction[None, :], axis=1) * scale_seq
    second_part = jnp.einsum("lf,bl->fb", hidden, grad_raw, precision=HIGH) * scale_seq
    grad_second, grad_decay, grad_skip = (
        lax.all_gather(second_part, "seq", axis=1, tiled=True),
        lax.all_gather(decay_part, "seq", axis=0, tiled=True),
        lax.all_gather(skip_part, "seq", axis=0, tiled=True),
    )
    hidden_part = jnp.einsum("bl,fb->lf", grad_raw, w_mine, precision=HIGH)
    cosine = jnp.cos(sine_input)
    grad_hidden = lax.psum(hidden_part, ("seq", "tp"))
    grad_first = (
        jnp.dot(
            positional.T, grad_hidden * cosine, precision=HIGH, preferred_element_type=jnp.float32
        )
        * scale_seq
    )
    grad_q = (grad_out.astype(jnp.float32) * to_rows(conv_back).astype(jnp.float32)).astype(
        jnp.bfloat16
    )
    grad_rows = to_rows(grad_back).astype(jnp.float32)
    grad_k = (grad_rows * v_proj.astype(jnp.float32)).astype(jnp.bfloat16)
    grad_v = (grad_rows * k_proj.astype(jnp.float32)).astype(jnp.bfloat16)
    return (grad_q, grad_k, grad_v, grad_first, grad_second, grad_decay, grad_skip)


def solution(mesh):
    return jax.shard_map(
        per_device,
        mesh=mesh,
        in_specs=(
            P("seq", "tp"),
            P("seq", "tp"),
            P("seq", "tp"),
            P("seq", "tp"),
            P(),
            P(None, "tp"),
            P("tp"),
            P("tp"),
        ),
        out_specs=(
            P("seq", "tp"),
            P("seq", "tp"),
            P("seq", "tp"),
            P(),
            P(None, "tp"),
            P("tp"),
            P("tp"),
        ),
        check_vma=False,
    )
```

profile of v0, /device:TPU:1, one launch (start us, length us, event | category | flops | bytes accessed | tf_op | source)
XLA Modules:
  0.0 877.4 jit_solution(5537863487157935746)
XLA Ops:
  7.2 1.2 copy.185
  8.4 1.2 copy.201
  10.4 19.8 %all-to-all-start.2 = ((bf16[64,16,128]{2,1,0:T(8,128)(2,1)}), bf16[64,16,128]{2,1,0:T(8,128)(2,1)S(1)}, u32[]{:S(2)}, u32[]{:S(2)}) async-start(bf16[64,16,128]{2,1,0:T(8,128)(2,1)} %bitcast.18), calls=%async_computation.2 | async-start | bytes 524288 | tf_op jit(solution)/shard_map/all_to_all | solution.py:147
  30.2 2.1 fusion.77
  33.1 10.8 %fusion.125 = (f32[8192,64]{0,1:T(8,128)S(1)}, f32[8192,64]{0,1:T(8,128)}) fusion(f32[32,64]{1,0:T(8,128)S(1)} %copy-done.38, f32[8192,16]{0,1:T(8,128)S(1)} %get-tuple-element.79, f32[8192,16]{0,1:T(8,128)S(1)} %get-tuple-element.78), kind=kOutput, calls=%fused_computation.169 | convolution fusion | flops 201588736 | bytes 5251072 | tf_op jit(solution)/shard_map/dot_general | solution.py:122
  44.0 1.2 fusion.104
  49.6 1.8 convolution_bitcast_fusion.2
  51.5 2.5 all-to-all-done.2
  54.0 1.9 convolution_bitcast_fusion
  56.5 3.4 fusion
  60.0 3.9 fusion.16
  65.3 2.0 fusion.20
  68.2 3.0 fusion.45
  71.2 1.9 div.36
  75.1 1.9 add_convert_fusion
  77.0 8.3 copy.210
  85.8 46.6 %reduce.1 = bf16[8192,16]{1,0:T(8,128)(2,1)} reduce(bf16[8192,1,16]{2,1,0:T(2,128)(2,1)} %bitcast.114, bf16[]{:T(256)} %broadcast.273), dimensions={1}, to_apply=%bitcast.107.reduce_sub_computation | reduce | bytes 524290
  132.4 4.4 reshape.244
  136.8 12.6 %all-to-all-start.3 = ((bf16[64,2,1024]{2,1,0:T(2,128)(2,1)}), bf16[64,2,1024]{2,1,0:T(2,128)(2,1)S(1)}, u32[]{:S(2)}, u32[]{:S(2)}) async-start(bf16[64,2,1024]{2,1,0:T(2,128)(2,1)} %reshape.244), calls=%async_computation.3 | async-start | bytes 524288 | tf_op jit(solution)/shard_map/all_to_all | solution.py:162
  150.3 1.8 copy.189
  152.1 21.2 %all-to-all-done.3 = bf16[64,2,1024]{2,1,0:T(2,128)(2,1)S(1)} async-done(((bf16[64,2,1024]{2,1,0:T(2,128)(2,1)}), bf16[64,2,1024]{2,1,0:T(2,128)(2,1)S(1)}, u32[]{:S(2)}, u32[]{:S(2)}) %all-to-all-start.3) | async-done | bytes 262176 | tf_op jit(solution)/shard_map/all_to_all | solution.py:162
  173.2 7.6 reshape.245
  180.8 8.6 copy.211
  191.9 4.5 all-to-all-start
  196.4 1.3 dynamic-slice
  198.3 1.8 copy.219
  200.1 1.8 copy.220
  201.9 17.9 %all-to-all-done = bf16[64,16,128]{2,1,0:T(8,128)(2,1)S(1)} async-done(((bf16[64,16,128]{2,1,0:T(8,128)(2,1)}), bf16[64,16,128]{2,1,0:T(8,128)(2,1)S(1)}, u32[]{:S(2)}, u32[]{:S(2)}) %all-to-all-start) | async-done | bytes 262176 | tf_op jit(solution)/shard_map/all_to_all | solution.py:133
  219.8 1.8 convolution_bitcast_fusion.1
  222.5 3.6 fusion.4
  227.0 2.0 fusion.8
  229.1 2.0 fusion.28
  231.1 1.8 multiply_subtract_fusion
  232.9 2.2 fusion.39
  235.1 2.3 convolution_multiply_fusion
  237.4 74.5 %all_gather.9 = f32[64,1024]{0,1:T(8,128)S(1)} all-gather(f32[64,16]{0,1:T(8,128)S(1)} %convolution_multiply_fusion), channel_id=1, replica_groups=mesh['seq'=64,'tp'=8] {'seq'}, dimensions={1}, use_global_device_ids=true | all-gather | bytes 266240 | tf_op jit(solution)/shard_map/all_gather | solution.py:168
  312.9 3.4 fusion.51
  316.7 6.7 copy.198
  323.4 45.2 %reduce.2 = bf16[8192,16]{1,0:T(8,128)(2,1)S(1)} reduce(bf16[8192,1,16]{2,1,0:T(2,128)(2,1)} %bitcast.115, bf16[]{:T(256)} %broadcast.273), dimensions={1}, to_apply=%bitcast.105.reduce_sub_computation | reduce | bytes 524290
  368.6 2.9 reshape.242
  371.6 4.9 all-to-all-start.1
  376.5 3.3 fusion.102
  381.2 133.2 %all-reduce.2 = (f32[1024]{0:T(1024)}, f32[1024]{0:T(1024)}) all-reduce(f32[1024]{0:T(1024)S(1)} %multiply_dynamic-update-slice_fusion.1, f32[1024]{0:T(1024)S(1)} %multiply_dynamic-update-slice_fusion), channel_id=1, replica_groups=mesh['seq'=64,'tp'=8] {'seq'}, use_global_device_ids=true, to_apply=%add | all-reduce | flops 2048 | bytes 16384
  514.4 7.6 reshape.243
  522.0 8.6 copy.199
  533.0 1.8 copy.218
  534.8 325.0 %all-reduce.5.cloned.1.call-done = f32[8192,64]{0,1:T(8,128)} async-done(((f32[8192,64]{0,1:T(8,128)}), f32[8192,64]{0,1:T(8,128)}) %all-reduce.5.cloned.1.call-update) | async-done | bytes 2097168 | tf_op jit(solution)/shard_map/psum | solution.py:174
  859.8 10.5 %fusion.54 = f32[32,64]{1,0:T(8,128)} fusion(f32[8192,64]{0,1:T(8,128)} %all-reduce.5.cloned.1.call-done, f32[8192,64]{0,1:T(8,128)S(1)} %copy-done.5, f32[8192,16]{0,1:T(8,128)S(1)} %copy-done.7, f32[8192,16]{0,1:T(8,128)S(1)} %get-tuple-element.78), kind=kOutput, calls=%fused_computation.47 | convolution fusion | flops 202115072 | bytes 5251072 | tf_op jit(solution)/shard_map/dot_general | solution.py:176
  (124 shorter events, 21.3 us)
Async XLA Ops:
  7.2 36.8 %copy-start = (f32[64,1024]{1,0:T(8,128)S(1)}, f32[64,1024]{1,0:T(8,128)}, u32[]{:S(2)}) copy-start(f32[64,1024]{1,0:T(8,128)} %param.13) | copy-start | bytes 786436
  7.2 26.0 %copy-start.38 = (f32[32,64]{1,0:T(8,128)S(1)}, f32[32,64]{1,0:T(8,128)}, u32[]{:S(2)}) copy-start(f32[32,64]{1,0:T(8,128)} %param.12) | copy-start | bytes 24580
  8.4 21.8 %copy-start.15 = (bf16[128,1024]{0,1:T(8,128)(2,1)}, bf16[128,1024]{0,1:T(8,128)(2,1)S(1)}, u32[]{:S(2)}) copy-start(bf16[128,1024]{0,1:T(8,128)(2,1)S(1)} %copy.185) | copy-start | bytes 786436
  10.4 43.6 %all-to-all-start.2 = ((bf16[64,16,128]{2,1,0:T(8,128)(2,1)}), bf16[64,16,128]{2,1,0:T(8,128)(2,1)S(1)}, u32[]{:S(2)}, u32[]{:S(2)}) async-start(bf16[64,16,128]{2,1,0:T(8,128)(2,1)} %bitcast.18), calls=%async_computation.2 | async-start | bytes 524288 | tf_op jit(solution)/shard_map/all_to_all | solution.py:147
  30.2 15.0 %copy-start.29 = (f32[8192]{0:T(1024)}, f32[8192]{0:T(1024)S(1)}, u32[]{:S(2)}) copy-start(f32[8192]{0:T(1024)S(1)} %convert_multiply_fusion.5) | copy-start | bytes 98308
  32.3 11.6 %copy-start.6 = (f32[8192,16]{0,1:T(8,128)}, f32[8192,16]{0,1:T(8,128)S(1)}, u32[]{:S(2)}) copy-start(f32[8192,16]{0,1:T(8,128)S(1)} %get-tuple-element.79) | copy-start | bytes 1572868
  44.0 1.8 copy-start.3
  45.2 4.4 copy-start.8
  45.6 14.3 %copy-start.19 = (f32[128,128]{0,1:T(8,128)}, f32[128,128]{0,1:T(8,128)S(1)}, u32[]{:S(2)}) copy-start(f32[128,128]{0,1:T(8,128)S(1)} %get-tuple-element.84) | copy-start | bytes 196612
  45.8 3.8 copy-start.35
  45.8 3.8 copy-start.36
  46.9 13.1 %copy-start.23 = (f32[128,128]{0,1:T(8,128)}, f32[128,128]{0,1:T(8,128)S(1)}, u32[]{:S(2)}) copy-start(f32[128,128]{0,1:T(8,128)S(1)} %fusion.106) | copy-start | bytes 196612
  48.9 16.4 %copy-start.17 = (f32[128,128]{0,1:T(8,128)}, f32[128,128]{0,1:T(8,128)S(1)}, u32[]{:S(2)}) copy-start(f32[128,128]{0,1:T(8,128)S(1)} %get-tuple-element.86) | copy-start | bytes 196612
  48.9 16.4 %copy-start.21 = (f32[128,128]{0,1:T(8,128)}, f32[128,128]{0,1:T(8,128)S(1)}, u32[]{:S(2)}) copy-start(f32[128,128]{0,1:T(8,128)S(1)} %get-tuple-element.87) | copy-start | bytes 196612
  54.0 19.1 %copy-start.10 = (bf16[64,16,128]{2,1,0:T(8,128)(2,1)}, bf16[64,16,128]{2,1,0:T(8,128)(2,1)S(1)}, u32[]{:S(2)}) copy-start(bf16[64,16,128]{2,1,0:T(8,128)(2,1)S(1)} %all-to-all-done.2) | copy-start | bytes 786436
  54.0 1.9 copy-start.33
  63.9 1.3 copy-start.1
  65.3 2.1 copy-start.31
  67.3 0.8 copy-start.25
  132.4 17.0 %copy-start.37 = (bf16[128,1024]{1,0:T(8,128)(2,1)S(1)}, bf16[128,1024]{1,0:T(8,128)(2,1)}, u32[]{:S(2)}) copy-start(bf16[128,1024]{1,0:T(8,128)(2,1)} %param.9) | copy-start | bytes 786436
  136.8 36.4 %all-to-all-start.3 = ((bf16[64,2,1024]{2,1,0:T(2,128)(2,1)}), bf16[64,2,1024]{2,1,0:T(2,128)(2,1)S(1)}, u32[]{:S(2)}, u32[]{:S(2)}) async-start(bf16[64,2,1024]{2,1,0:T(2,128)(2,1)} %reshape.244), calls=%async_computation.3 | async-start | bytes 524288 | tf_op jit(solution)/shard_map/all_to_all | solution.py:162
  189.5 1.5 copy-start.27
  189.5 1.5 copy-start.28
  191.9 29.8 %copy-start.34 = (f32[128,128]{0,1:T(8,128)S(1)}, f32[128,128]{0,1:T(8,128)}, u32[]{:S(2)}) copy-start(f32[128,128]{0,1:T(8,128)} %get-tuple-element.82) | copy-start | bytes 196612
  191.9 27.9 %all-to-all-start = ((bf16[64,16,128]{2,1,0:T(8,128)(2,1)}), bf16[64,16,128]{2,1,0:T(8,128)(2,1)S(1)}, u32[]{:S(2)}, u32[]{:S(2)}) async-start(bf16[64,16,128]{2,1,0:T(8,128)(2,1)} %bitcast.127), calls=%async_computation | async-start | bytes 524288 | tf_op jit(solution)/shard_map/all_to_all | solution.py:133
  219.8 2.2 copy-start.12
  221.7 0.8 copy-start.20
  221.7 0.9 copy-start.24
  222.5 3.6 copy-start.2
  226.2 0.8 copy-start.18
  226.2 0.9 copy-start.22
  229.1 2.1 copy-start.32
  231.1 1.8 copy-start.26
  232.9 2.2 copy-start.4
  232.9 2.2 copy-start.30
  312.9 3.5 copy-start.13
  371.6 142.9 %all-to-all-start.1 = ((bf16[64,2,1024]{2,1,0:T(2,128)(2,1)}), bf16[64,2,1024]{2,1,0:T(2,128)(2,1)S(1)}, u32[]{:S(2)}, u32[]{:S(2)}) async-start(bf16[64,2,1024]{2,1,0:T(2,128)(2,1)} %reshape.242), calls=%async_computation.1 | async-start | bytes 524288 | tf_op jit(solution)/shard_map/all_to_all | solution.py:146
  376.4 3.4 copy-start.9
  376.4 483.4 %all-reduce.5.cloned.1.call-start = ((), (), s32[]{:S(2)}) async-start(), calls=%async_computation.4 | async-start | bytes 4194304 | tf_op jit(solution)/shard_map/psum | solution.py:174
  379.8 0.9 copy-start.11
  379.8 1.0 copy-start.14
  530.7 1.6 copy-start.16
  530.7 329.2 %copy-start.5 = (f32[8192,64]{0,1:T(8,128)S(1)}, f32[8192,64]{0,1:T(8,128)}, u32[]{:S(2)}) copy-start(f32[8192,64]{0,1:T(8,128)} %get-tuple-element.81) | copy-start | bytes 6291460
  530.7 329.2 %copy-start.7 = (f32[8192,16]{0,1:T(8,128)S(1)}, f32[8192,16]{0,1:T(8,128)}, u32[]{:S(2)}) copy-start(f32[8192,16]{0,1:T(8,128)} %copy-done.6) | copy-start | bytes 1572868
Sparse Core Ops, SparseCore 0:
  382.6 477.1 all-reduce.4
where the time goes:
time: 889 us; the launch traced here: 877 us
  waiting for transfers between devices  367 us (41%)
  blocking collectives  208 us (23%)
  other arithmetic  111 us (12%)
  local copies, waits for them, and re-layouts  75.7 us (9%)
  matrix products  59.4 us (7%)
  starting transfers between devices  41.8 us (5%)
  between operations  15.5 us (2%)
    psum x1, waiting for transfers between devices, per_device(): grad_hidden = lax.psum(hidden_part, ('seq', 'tp'))  325 us
    unnamed x1, blocking collectives  133 us
    unnamed x7, other arithmetic  94.3 us
    all_gather x1, blocking collectives, per_device(): lax.all_gather(second_part, 'seq', axis=1, tiled=True)  74.5 us
    unnamed x97, local copies, waits for them, and re-layouts  38.8 us
    all_to_all x1, waiting for transfers between devices, per_device(): lax.all_to_all(back_block, 'seq', split_axis=2, concat_axis=0, tiled=True)  21.2 us
    all_to_all x1, starting transfers between devices, per_device(): lax.all_to_all(to_channels(gated_grad), 'seq', split_axis=0, concat_axis=...  19.8 us
    all_to_all x1, waiting for transfers between devices, per_device(): lax.all_to_all(to_channels(gated_in), 'seq', split_axis=0, concat_axis=2,...  17.9 us
  transfers between devices with their start and end apart: 5, of which 4 were waited for; matrix products, arithmetic and copies ran while one was open for 6% of the time, Pallas kernels for 0%

commit v1 on v0

v1 whole, which is shorter than its diff:
```python
import functools
import math

import jax
import jax.numpy as jnp
import numpy as np
from jax import lax
from jax.experimental import pallas as pl
from jax.experimental.pallas import tpu as pltpu
from jax.sharding import PartitionSpec as P

MESH = pl.DeviceIdType.MESH
F32 = jnp.float32
BF16 = jnp.bfloat16
J = 64
B = 128
C = 16
L = J * B
GROUP = 4
SEQ = 64
TP = 8
DEPTH = 16
PLANE = 4


def split_np(values):
    high = values.astype(np.float32).astype(jnp.bfloat16)
    low = (values - high.astype(np.float64)).astype(np.float32).astype(jnp.bfloat16)
    return high, low


def make_tables():
    turn = 2.0 * math.pi
    k1 = np.arange(J)[:, None] + 0.25
    first = turn * k1 * np.arange(J)[None, :] / J
    f1_high, f1_low = split_np(np.concatenate([np.cos(first), -np.sin(first)], axis=0))
    twiddle = turn * k1 * np.arange(B)[None, :] / L
    second = turn * (np.arange(B)[:, None] * np.arange(B)[None, :] % B) / B
    cos, sin = np.cos(second), np.sin(second)
    f2_high, f2_low = split_np(np.block([[cos, -sin], [sin, cos]]))
    i1_high, i1_low = split_np(np.block([[cos, sin], [-sin, cos]]))
    i2_high, i2_low = split_np(np.concatenate([np.cos(first.T), -np.sin(first.T)], axis=1) / L)
    band = np.arange(16)
    freq = 3 * (band + 1) ** 2 + band
    inner = turn * (freq[:, None] * np.arange(B)[None, :] % L) / L
    p_high, p_low = split_np(np.concatenate([np.sin(inner), np.cos(inner)], axis=0))
    outer = turn * (np.arange(J)[:, None] * freq[None, :] % J) / J
    pos_t = np.zeros((3 * B, B), np.float32).astype(jnp.bfloat16)
    for at, part in enumerate((p_high, p_high, p_low)):
        pos_t[at * B : (at + 1) * B, :32] = part.T
    turn_cos = np.tile(np.concatenate([np.cos(outer), np.cos(outer)], axis=1), (1, 4))
    turn_sin = np.tile(np.concatenate([-np.sin(outer), np.sin(outer)], axis=1), (1, 4))
    return (
        np.concatenate([f1_high, f1_low], axis=1),
        np.concatenate([f1_high, f1_low, f1_high], axis=1),
        np.concatenate([f2_high, f2_high, f2_low], axis=0),
        np.concatenate([i1_high, i1_high, i1_low], axis=0),
        np.concatenate([i2_high, i2_low, i2_high], axis=1),
        np.cos(twiddle).astype(np.float32),
        np.sin(twiddle).astype(np.float32),
        np.concatenate([p_high, p_low, p_high, p_low], axis=0),
        pos_t,
        turn_cos.astype(np.float32),
        turn_sin.astype(np.float32),
    )


def dot(left, right):
    return jnp.dot(left, right, preferred_element_type=F32)


def split(values):
    high = values.astype(BF16)
    return high, (values - high.astype(F32)).astype(BF16)


def sin_cos(x):
    n = jnp.floor(x * (1.0 / math.pi) + 0.5)
    r = (x - n * 3.140625) - n * 9.6765358979e-4
    half = n * 0.5
    sign = 1.0 - 4.0 * (half - jnp.floor(half))
    s = r * r
    p = -1.0 / 39916800.0
    for factor in (1.0 / 362880.0, -1.0 / 5040.0, 1.0 / 120.0, -1.0 / 6.0):
        p = p * s + factor
    sine = (r + r * s * p) * sign
    q = 1.0 / 479001600.0
    for factor in (-1.0 / 3628800.0, 1.0 / 40320.0, -1.0 / 720.0, 1.0 / 24.0, -0.5, 1.0):
        q = q * s + factor
    return sine, q * sign


def kernel(
    q_ref, k_ref, v_ref, go_ref, w1_ref, w2_ref, decay_ref, skip_ref,
    f1x_ref, f1_ref, f2_ref, i1_ref, i2_ref, twc_ref, tws_ref, pb_ref, pt_ref, tc_ref, ts_ref,
    gq_ref, gk_ref, gv_ref, first_ref, second_ref, gdecay_ref, gskip_ref,
    send_x, send_g, in_x, in_g, back_x, back_g, conv_in, grad_in,
    params, stage, stage_x, raw_ref, env_ref, hid_hi, hid_lo, cos_ref, spec_h, spec_x, spec_g, wide,
    gather, rs_out, rs_in, plane_in, tp_in, fin,
    send_sem, x_sem, g_sem, cx_sem, cg_sem, z_sem, rz_sem, y_sem, ry_sem, t_sem, f_sem,
):
    me = lax.axis_index("seq")
    my_tp = lax.axis_index("tp")
    my_z, my_y = me // PLANE, me % PLANE
    scale = L**-0.5

    barrier = pltpu.get_barrier_semaphore()

    def greet(i, carry):
        pl.semaphore_signal(
            barrier, inc=1, device_id={"seq": (me + i) % SEQ}, device_id_type=MESH
        )
        return carry

    lax.fori_loop(1, SEQ, greet, 0)

    def greet_tp(i, carry):
        pl.semaphore_signal(
            barrier, inc=1, device_id={"tp": (my_tp + i) % TP}, device_id_type=MESH
        )
        return carry

    lax.fori_loop(1, TP, greet_tp, 0)

    def gate(left_ref, right_ref, out_ref):
        def step(at, carry):
            parts = []
            for half in range(2):
                lanes = pl.ds(pl.multiple_of(half * 512 + at * B, B), B)
                gated = left_ref[:, lanes].astype(F32) * right_ref[:, lanes].astype(F32)
                parts.append(jnp.transpose(gated).reshape(16, 8, B))
            out_ref[pl.ds(at * 16, 16)] = jnp.concatenate(parts, axis=1).astype(BF16)
            return carry

        lax.fori_loop(0, 4, step, 0)

    def exchange(out_ref, in_ref, recv_sem, send_at):
        def step(i, carry):
            for peer in ((me + i) % SEQ, (me + SEQ - i) % SEQ):
                pltpu.make_async_remote_copy(
                    src_ref=out_ref.at[peer],
                    dst_ref=in_ref.at[me],
                    send_sem=send_sem.at[send_at],
                    recv_sem=recv_sem,
                    device_id={"seq": peer},
                    device_id_type=MESH,
                ).start()
            return carry

        lax.fori_loop(1, SEQ // 2, step, 0)
        peer = (me + SEQ // 2) % SEQ
        pltpu.make_async_remote_copy(
            src_ref=out_ref.at[peer],
            dst_ref=in_ref.at[me],
            send_sem=send_sem.at[send_at],
            recv_sem=recv_sem,
            device_id={"seq": peer},
            device_id_type=MESH,
        ).start()
        in_ref[me] = out_ref[me]

    def wait_bytes(ref, count, sem):
        view = ref.at[pl.ds(0, count)]
        pltpu.make_async_copy(view, view, sem).wait()

    gate(k_ref, v_ref, send_x)
    pl.semaphore_wait(barrier, SEQ - 1 + TP - 1)
    exchange(send_x, in_x, x_sem, 0)
    gate(q_ref, go_ref, send_g)
    exchange(send_g, in_g, g_sem, 1)

    for half in range(2):
        lanes = pl.ds(pl.multiple_of(half * 512 + (me // 16) * B, B), B)
        rows = lax.broadcasted_iota(jnp.int32, (64, B), 0)
        tail = jnp.where(
            rows == 0,
            jnp.broadcast_to(decay_ref[:, lanes], (64, B)),
            jnp.where(rows == 1, jnp.broadcast_to(skip_ref[:, lanes], (64, B)), 0.0),
        )
        params[half] = jnp.transpose(jnp.concatenate([w2_ref[:, lanes], tail], axis=0))
    pick = pl.ds(pl.multiple_of((me % 16) * 8, 8), 8)
    mine = jnp.concatenate([params[0, pick, :], params[1, pick, :]], axis=0)
    lane = lax.broadcasted_iota(jnp.int32, (C, B), 1)
    weights = jnp.where(lane < 64, mine, 0.0)
    decay = jnp.sum(jnp.where(lane == 64, mine, 0.0), axis=1, keepdims=True)
    skip = jnp.sum(jnp.where(lane == 65, mine, 0.0), axis=1, keepdims=True)
    w_high = weights.astype(BF16).astype(F32)
    w_low = (weights - w_high).astype(BF16).astype(F32)
    w_pair = w_high + pltpu.roll(w_low, 64, 1)
    w_rows = jnp.concatenate([w_pair, w_pair], axis=1).astype(BF16)
    wide[...] = jnp.zeros((B, B), F32)
    for at, part in enumerate((w_high, w_low, w_high, w_low)):
        wide[at * C : (at + 1) * C, :] = part
    w_cols = jnp.transpose(wide[...])[:64, :64].astype(BF16)

    w_one = w1_ref[...]
    w_swap = jnp.concatenate([w_one[16:], w_one[:16]], axis=0)
    wide[:, :64] = jnp.concatenate([w_one] * 4, axis=0)
    turned = jnp.transpose(wide[...])[:64]
    wide[:, :64] = jnp.concatenate([w_swap] * 4, axis=0)
    turned_swap = jnp.transpose(wide[...])[:64]
    lane_b = lax.broadcasted_iota(jnp.int32, (GROUP * 64, B), 1)
    position = lax.broadcasted_iota(jnp.int32, (C, B), 1).astype(F32)

    def network(at, carry):
        pieces = []
        for i in range(GROUP):
            j = at * GROUP + i
            pieces.append(turned * tc_ref[pl.ds(j, 1), :] + turned_swap * ts_ref[pl.ds(j, 1), :])
        values = jnp.concatenate(pieces, axis=0)
        high = values.astype(BF16).astype(F32)
        left = jnp.where(lane_b < 64, high, values - high).astype(BF16)
        sine, cosine = sin_cos(dot(left, pb_ref[...]))
        rows = pl.ds(pl.multiple_of(at * GROUP * 64, GROUP * 64), GROUP * 64)
        cos_ref[rows, :] = cosine
        high, low = split(sine)
        hid_hi[rows, :] = high
        hid_lo[rows, :] = low
        for i in range(0, GROUP, 2):
            h = jnp.concatenate([high[i * 64 : (i + 1) * 64], high[(i + 1) * 64 : (i + 2) * 64]], axis=1)
            l = jnp.concatenate([low[i * 64 : (i + 1) * 64], low[(i + 1) * 64 : (i + 2) * 64]], axis=1)
            raw = dot(w_rows, jnp.concatenate([h, h, l, l], axis=0))
            for o in range(2):
                j = at * GROUP + i + o
                fraction = (position + (j * B).astype(F32)) * (1.0 / L)
                envelope = jnp.exp(-decay * fraction) * scale
                part = raw[:, o * B : (o + 1) * B]
                here = pl.ds(pl.multiple_of(j * C, C), C)
                raw_ref[here, :] = part
                env_ref[here, :] = envelope
                stage[here, :] = part * envelope
        return carry

    lax.fori_loop(0, J // GROUP, network, 0)

    def forward(from_ref, spec_ref, exact):
        def step(at, carry):
            cols = [from_ref[pl.ds(at * GROUP + i, J, stride=C), :] for i in range(GROUP)]
            data = jnp.concatenate(cols, axis=1)
            if exact:
                data = data.astype(BF16)
                mixed = dot(f1x_ref[...], jnp.concatenate([data, data], axis=0))
            else:
                high, low = split(data)
                mixed = dot(f1_ref[...], jnp.concatenate([high, high, low], axis=0))
            turned = []
            for i in range(GROUP):
                re, im = mixed[:J, i * B : (i + 1) * B], mixed[J:, i * B : (i + 1) * B]
                c, s = twc_ref[...], tws_ref[...]
                turned.append(jnp.concatenate([re * c + im * s, im * c - re * s], axis=1))
            high, low = split(jnp.concatenate(turned, axis=0))
            rows = pl.ds(pl.multiple_of(at * GROUP * J, GROUP * J), GROUP * J)
            spec_ref[rows, :] = dot(jnp.concatenate([high, low, high], axis=1), f2_ref[...])
            return carry

        lax.fori_loop(0, C // GROUP, step, 0)

    def inverse(left_ref, right_ref, conjugate):
        def step(at, carry):
            rows = pl.ds(pl.multiple_of(at * GROUP * J, GROUP * J), GROUP * J)
            a, b = left_ref[rows, :], right_ref[rows, :]
            ar, ai, br, bi = a[:, :B], a[:, B:], b[:, :B], b[:, B:]
            if conjugate:
                product = jnp.concatenate([ar * br + ai * bi, ar * bi - ai * br], axis=1)
            else:
                product = jnp.concatenate([ar * br - ai * bi, ar * bi + ai * br], axis=1)
            high, low = split(product)
            mixed = dot(jnp.concatenate([high, low, high], axis=1), i1_ref[...])
            turned = []
            for i in range(GROUP):
                re, im = mixed[i * J : (i + 1) * J, :B], mixed[i * J : (i + 1) * J, B:]
                c, s = twc_ref[...], tws_ref[...]
                turned.append(jnp.concatenate([re * c - im * s, re * s + im * c], axis=0))
            high, low = split(jnp.concatenate(turned, axis=1))
            result = dot(i2_ref[...], jnp.concatenate([high, high, low], axis=0))
            for i in range(GROUP):
                stage[pl.ds(at * GROUP + i, J, stride=C), :] = result[:, i * B : (i + 1) * B]
            return carry

        lax.fori_loop(0, C // GROUP, step, 0)

    def finish(in_ref, out_ref):
        def step(at, carry):
            blocks = pl.ds(at * 8, 8)
            rows = pl.ds(pl.multiple_of(at * 8 * C, 8 * C), 8 * C)
            values = stage[rows, :].reshape(8, C, B) + skip[None] * in_ref[blocks].astype(F32)
            out_ref[blocks] = values.astype(BF16)
            return carry

        lax.fori_loop(0, J // 8, step, 0)

    def widen(in_ref, to_ref):
        def step(at, carry):
            rows = pl.ds(pl.multiple_of(at * 8 * C, 8 * C), 8 * C)
            to_ref[rows, :] = in_ref[pl.ds(at * 8, 8)].astype(F32).reshape(8 * C, B)
            return carry

        lax.fori_loop(0, J // 8, step, 0)

    forward(stage, spec_h, False)
    wait_bytes(in_x, SEQ - 1, x_sem)
    widen(in_x, stage_x)
    forward(stage_x, spec_x, True)
    inverse(spec_h, spec_x, False)
    finish(in_x, back_x)
    exchange(back_x, conv_in, cx_sem, 2)

    wait_bytes(in_g, SEQ - 1, g_sem)
    widen(in_g, stage)
    forward(stage, spec_g, True)
    inverse(spec_h, spec_g, True)
    finish(in_g, back_g)
    exchange(back_g, grad_in, cg_sem, 3)

    inverse(spec_x, spec_g, True)

    def reduce_filter(at, carry):
        decay_sum, skip_sum, second, cos_sum, sin_sum = carry
        left, right, hid_rows = [], [], []
        for i in range(GROUP):
            j = at * GROUP + i
            here = pl.ds(pl.multiple_of(j * C, C), C)
            grad_raw = stage[here, :] * env_ref[here, :]
            fraction = (position + (j * B).astype(F32)) * (1.0 / L)
            decay_sum += grad_raw * raw_ref[here, :] * fraction
            skip_sum += in_x[j].astype(F32) * in_g[j].astype(F32)
            high, low = split(grad_raw)
            right.append(jnp.concatenate([high, high, low], axis=1))
            rows = pl.ds(pl.multiple_of(j * 64, 64), 64)
            h = hid_hi[rows, :]
            hid_rows.append(jnp.concatenate([h, hid_lo[rows, :], h], axis=1))
            left.append(dot(w_cols, jnp.concatenate([high, high, low, low], axis=0)))
        second += lax.dot_general(
            jnp.concatenate(hid_rows, axis=1),
            jnp.concatenate(right, axis=1),
            (((1,), (1,)), ((), ())),
            preferred_element_type=F32,
        )
        rows = pl.ds(pl.multiple_of(at * GROUP * 64, GROUP * 64), GROUP * 64)
        high, low = split(jnp.concatenate(left, axis=0) * cos_ref[rows, :])
        turned = dot(jnp.concatenate([high, low, high], axis=1), pt_ref[...])
        for i in range(GROUP):
            j = at * GROUP + i
            part = turned[i * 64 : (i + 1) * 64]
            cos_sum += part * tc_ref[pl.ds(j, 1), :]
            sin_sum += part * ts_ref[pl.ds(j, 1), :]
        return decay_sum, skip_sum, second, cos_sum, sin_sum

    zero = jnp.zeros((C, B), F32)
    decay_sum, skip_sum, second, cos_sum, sin_sum = lax.fori_loop(
        0,
        J // GROUP,
        reduce_filter,
        (zero, zero, jnp.zeros((64, C), F32), jnp.zeros((64, B), F32), jnp.zeros((64, B), F32)),
    )
    wide[...] = jnp.zeros((B, B), F32)
    wide[:64, :C] = second * scale
    packed = jnp.transpose(wide[...])[:C]
    packed = jnp.where(lane == 64, -scale * jnp.sum(decay_sum, axis=1, keepdims=True), packed)
    packed = jnp.where(lane == 65, scale * jnp.sum(skip_sum, axis=1, keepdims=True), packed)
    gather[my_z, my_y] = packed.astype(BF16)

    lane_64 = lax.broadcasted_iota(jnp.int32, (64, B), 1)
    swapped = jnp.where(lane_64 < 16, pltpu.roll(sin_sum, B - 16, 1), pltpu.roll(sin_sum, 16, 1))
    wide[:64, :] = (cos_sum + swapped) * scale
    wide[64:, :] = jnp.zeros((64, B), F32)
    first = jnp.transpose(wide[...])
    first = jnp.where(lane < 64, first[:16], pltpu.roll(first[16:32], 64, 1))
    for i in range(DEPTH):
        rs_out[i] = first[i : i + 1]
    rs_in[my_z] = rs_out[my_z]

    def send_z(i, carry):
        peer = (my_z + i) % DEPTH
        pltpu.make_async_remote_copy(
            src_ref=rs_out.at[peer],
            dst_ref=rs_in.at[my_z],
            send_sem=send_sem.at[4],
            recv_sem=rz_sem,
            device_id={"seq": peer * PLANE + my_y},
            device_id_type=MESH,
        ).start()
        pltpu.make_async_remote_copy(
            src_ref=gather.at[my_z, my_y],
            dst_ref=gather.at[my_z, my_y],
            send_sem=send_sem.at[5],
            recv_sem=z_sem,
            device_id={"seq": peer * PLANE + my_y},
            device_id_type=MESH,
        ).start()
        return carry

    lax.fori_loop(1, DEPTH, send_z, 0)

    def to_rows(in_ref, at, half):
        block = in_ref[pl.ds(at * 16, 16)].astype(F32)[:, half * 8 : (half + 1) * 8]
        return jnp.transpose(block.reshape(B, B))

    wait_bytes(conv_in, SEQ - 1, cx_sem)

    def rows_q(at, carry):
        for half in range(2):
            lanes = pl.ds(pl.multiple_of(half * 512 + at * B, B), B)
            gq_ref[:, lanes] = (go_ref[:, lanes].astype(F32) * to_rows(conv_in, at, half)).astype(BF16)
        return carry

    lax.fori_loop(0, 4, rows_q, 0)

    wait_bytes(rs_in, DEPTH - 1, rz_sem)
    total = rs_in[0]
    for i in range(1, DEPTH):
        total += rs_in[i]
    plane_in[my_y] = total

    def send_plane(i, carry):
        peer = (my_y + i) % PLANE
        pltpu.make_async_remote_copy(
            src_ref=plane_in.at[my_y],
            dst_ref=plane_in.at[my_y],
            send_sem=send_sem.at[6],
            recv_sem=ry_sem,
            device_id={"seq": my_z * PLANE + peer},
            device_id_type=MESH,
        ).start()
        return carry

    lax.fori_loop(1, PLANE, send_plane, 0)
    wait_bytes(gather.at[:, 0], DEPTH - 1, z_sem)

    def send_gather(i, carry):
        peer = (my_y + i) % PLANE
        pltpu.make_async_remote_copy(
            src_ref=gather.at[:, my_y],
            dst_ref=gather.at[:, my_y],
            send_sem=send_sem.at[7],
            recv_sem=y_sem,
            device_id={"seq": my_z * PLANE + peer},
            device_id_type=MESH,
        ).start()
        return carry

    lax.fori_loop(1, PLANE, send_gather, 0)
    wait_bytes(plane_in, PLANE - 1, ry_sem)
    total = plane_in[0]
    for i in range(1, PLANE):
        total += plane_in[i]
    tp_in[my_tp] = total

    def send_tp(i, carry):
        pltpu.make_async_remote_copy(
            src_ref=tp_in.at[my_tp],
            dst_ref=tp_in.at[my_tp],
            send_sem=send_sem.at[8],
            recv_sem=t_sem,
            device_id={"tp": (my_tp + i) % TP},
            device_id_type=MESH,
        ).start()
        return carry

    lax.fori_loop(1, TP, send_tp, 0)
    wait_bytes(tp_in, TP - 1, t_sem)
    total = tp_in[0]
    for i in range(1, TP):
        total += tp_in[i]
    fin[my_z] = total

    def send_fin(i, carry):
        peer = (my_z + i) % DEPTH
        pltpu.make_async_remote_copy(
            src_ref=fin.at[my_z],
            dst_ref=fin.at[my_z],
            send_sem=send_sem.at[9],
            recv_sem=f_sem,
            device_id={"seq": peer * PLANE + my_y},
            device_id_type=MESH,
        ).start()
        return carry

    lax.fori_loop(1, DEPTH, send_fin, 0)

    wait_bytes(grad_in, SEQ - 1, cg_sem)

    def rows_kv(at, carry):
        for half in range(2):
            lanes = pl.ds(pl.multiple_of(half * 512 + at * B, B), B)
            grad = to_rows(grad_in, at, half)
            gk_ref[:, lanes] = (v_ref[:, lanes].astype(F32) * grad).astype(BF16)
            gv_ref[:, lanes] = (k_ref[:, lanes].astype(F32) * grad).astype(BF16)
        return carry

    lax.fori_loop(0, 4, rows_kv, 0)

    others = gather.at[:, pl.ds(0, PLANE - 1)]
    pltpu.make_async_copy(others, others, y_sem).wait()

    def columns(at, carry):
        for half in range(2):
            lanes = pl.ds(pl.multiple_of(half * 512 + at * B, B), B)
            block = gather[pl.ds(at * 4, 4)].astype(F32).reshape(16, C, B)[:, half * 8 : (half + 1) * 8]
            turned = jnp.transpose(block.reshape(B, B))
            second_ref[:, lanes] = turned[:64]
            gdecay_ref[:, lanes] = turned[64:65]
            gskip_ref[:, lanes] = turned[65:66]
        return carry

    lax.fori_loop(0, 4, columns, 0)

    wait_bytes(fin, DEPTH - 1, f_sem)
    for i in range(DEPTH):
        wide[i : i + 1, :] = fin[i]
    total = wide[:DEPTH, :]
    first_ref[:16, :] = total[:, :64]
    first_ref[16:, :] = pltpu.roll(total, 64, 1)[:, :64]

    for at, ref in enumerate((send_x, send_g, back_x, back_g)):
        wait_bytes(ref, SEQ - 1, send_sem.at[at])
    wait_bytes(rs_out, DEPTH - 1, send_sem.at[4])
    wait_bytes(gather.at[:, 0], DEPTH - 1, send_sem.at[5])
    wait_bytes(plane_in, PLANE - 1, send_sem.at[6])
    pltpu.make_async_copy(others, others, send_sem.at[7]).wait()
    wait_bytes(tp_in, TP - 1, send_sem.at[8])
    wait_bytes(fin, DEPTH - 1, send_sem.at[9])


def per_device(q_proj, k_proj, v_proj, grad_out, w_first, w_second, decay_rate, skip_gain):
    chan = decay_rate.shape[0]
    tables = [jnp.asarray(table) for table in make_tables()]
    rows = jax.ShapeDtypeStruct(q_proj.shape, BF16)
    block = pltpu.VMEM((J, C, B), BF16)
    full = pltpu.VMEM((J * C, B), F32)
    spectrum = pltpu.VMEM((C * J, 2 * B), F32)
    dma = pltpu.SemaphoreType.DMA
    vmem = pl.BlockSpec(memory_space=pltpu.VMEM)
    grad_q, grad_k, grad_v, first, second, decay, skip = pl.pallas_call(
        kernel,
        out_shape=(
            rows,
            rows,
            rows,
            jax.ShapeDtypeStruct(w_first.shape, F32),
            jax.ShapeDtypeStruct(w_second.shape, F32),
            jax.ShapeDtypeStruct((1, chan), F32),
            jax.ShapeDtypeStruct((1, chan), F32),
        ),
        in_specs=[vmem] * (8 + len(tables)),
        out_specs=[vmem] * 7,
        scratch_shapes=[block] * 8
        + [pltpu.VMEM((2, B, B), F32)]
        + [full] * 4
        + [pltpu.VMEM((J * 64, B), BF16)] * 2
        + [pltpu.VMEM((J * 64, B), F32)]
        + [spectrum] * 3
        + [pltpu.VMEM((B, B), F32)]
        + [pltpu.VMEM((DEPTH, PLANE, C, B), BF16)]
        + [pltpu.VMEM((count, 1, B), F32) for count in (DEPTH, DEPTH, PLANE, TP, DEPTH)]
        + [dma((10,))]
        + [dma(())] * 10,
        compiler_params=pltpu.CompilerParams(
            collective_id=0, has_side_effects=True, vmem_limit_bytes=48 * 1024 * 1024
        ),
    )(
        q_proj, k_proj, v_proj, grad_out, w_first, w_second,
        decay_rate.reshape(1, chan), skip_gain.reshape(1, chan), *tables,
    )
    return grad_q, grad_k, grad_v, first, second, decay.reshape(chan), skip.reshape(chan)


def solution(mesh):
    return jax.shard_map(
        per_device,
        mesh=mesh,
        in_specs=(
            P("seq", "tp"),
            P("seq", "tp"),
            P("seq", "tp"),
            P("seq", "tp"),
            P(),
            P(None, "tp"),
            P("tp"),
            P("tp"),
        ),
        out_specs=(
            P("seq", "tp"),
            P("seq", "tp"),
            P("seq", "tp"),
            P(),
            P(None, "tp"),
            P("tp"),
            P("tp"),
        ),
        check_vma=False,
    )
```

time: 889 us -> 108 us (0.12)
  the two profiles are of different devices: /device:TPU:1 before, /device:TPU:16 now
where the time goes in v1:
time: 108 us; the launch traced here: 107 us
  Pallas kernels  86.1 us (80%)
  local copies, waits for them, and re-layouts  20.5 us (19%)
    pallas_call x1, Pallas kernels, per_device(): pl.pallas_call(kernel, out_shape=(rows, rows, rows, jax.ShapeDtypeStruct(...  86.1 us
    unnamed x45, local copies, waits for them, and re-layouts  20.5 us

profile of v1, /device:TPU:16, one launch (start us, length us, event | category | flops | bytes accessed | tf_op | source)
XLA Modules:
  0.0 107.2 jit_solution(2591808685222197727)
XLA Ops:
  0.6 0.0 copy-start
  0.6 1.0 copy-done
  1.6 0.0 copy-start.1
  1.6 1.0 copy-done.1
  2.6 0.0 copy-start.2
  2.6 0.9 copy-done.2
  3.6 0.0 copy-start.3
  3.6 0.9 copy-done.3
  4.5 0.0 copy-start.4
  4.5 0.9 copy-done.4
  5.5 0.0 copy-start.5
  5.5 0.9 copy-done.5
  6.4 0.0 copy-start.6
  6.4 0.9 copy-done.6
  7.4 0.0 copy-start.7
  7.4 0.9 copy-done.7
  8.3 0.0 copy-start.8
  8.3 0.8 copy-done.8
  9.1 0.0 copy-start.9
  9.1 0.8 copy-done.9
  9.9 0.0 copy-start.10
  9.9 0.8 copy-done.10
  10.7 0.0 copy-start.11
  10.7 0.8 copy-done.11
  11.4 0.0 copy-start.12
  11.4 0.8 copy-done.12
  12.2 0.0 copy-start.13
  12.2 0.8 copy-done.13
  12.9 0.0 copy-start.14
  13.0 0.8 copy-done.14
  13.7 0.0 copy-start.15
  13.7 0.8 copy-done.15
  14.5 0.0 copy-start.16
  14.5 0.7 copy-done.16
  15.2 0.0 copy-start.17
  15.2 0.7 copy-done.17
  15.9 0.0 copy-start.18
  15.9 0.7 copy-done.18
  16.6 86.1 %shard_map.234 = (bf16[128,1024]{1,0:T(8,128)(2,1)S(1)}, bf16[128,1024]{1,0:T(8,128)(2,1)S(1)}, bf16[128,1024]{1,0:T(8,128)(2,1)S(1)}, f32[32,64]{1,0:T(8,128)S(...) custom-call(bf16[128,1024]{1,0:T(8,128)(2,1)S(1)} %copy-done.2, ...), custom_call_target="tpu_custom_call" | custom-call | tf_op jit(solution)/shard_map/pallas_call | solution.py:534
  102.6 0.7 copy.33
  103.3 0.7 copy.34
  104.0 0.7 copy.35
  104.8 0.6 copy.36
  105.4 0.7 copy.37
  106.1 0.6 copy.38
  106.7 0.6 copy.39
Async XLA Ops:
  0.6 1.0 copy-start
  1.6 1.0 copy-start.1
  2.6 0.9 copy-start.2
  3.6 0.9 copy-start.3
  4.5 0.9 copy-start.4
  5.5 0.9 copy-start.5
  6.4 0.9 copy-start.6
  7.4 0.9 copy-start.7
  8.3 0.8 copy-start.8
  9.1 0.8 copy-start.9
  9.9 0.8 copy-start.10
  10.7 0.8 copy-start.11
  11.4 0.8 copy-start.12
  12.2 0.8 copy-start.13
  12.9 0.8 copy-start.14
  13.7 0.8 copy-start.15
  14.5 0.7 copy-start.16
  15.2 0.7 copy-start.17
  15.9 0.7 copy-start.18

commit v2 on v1

--- a/solution.py
+++ b/solution.py
@@ -19,6 +19,7 @@
 GROUP = 4
 SEQ = 64
 TP = 8
+OPERANDS = 16
 DEPTH = 16
 PLANE = 4
 
@@ -56,12 +57,9 @@
         np.concatenate([f2_high, f2_high, f2_low], axis=0),
         np.concatenate([i1_high, i1_high, i1_low], axis=0),
         np.concatenate([i2_high, i2_low, i2_high], axis=1),
-        np.cos(twiddle).astype(np.float32),
-        np.sin(twiddle).astype(np.float32),
         np.concatenate([p_high, p_low, p_high, p_low], axis=0),
         pos_t,
-        turn_cos.astype(np.float32),
-        turn_sin.astype(np.float32),
+        np.stack([np.cos(twiddle), np.sin(twiddle), turn_cos, turn_sin]).astype(np.float32),
     )
 
 
@@ -90,15 +88,32 @@
     return sine, q * sign
 
 
-def kernel(
-    q_ref, k_ref, v_ref, go_ref, w1_ref, w2_ref, decay_ref, skip_ref,
-    f1x_ref, f1_ref, f2_ref, i1_ref, i2_ref, twc_ref, tws_ref, pb_ref, pt_ref, tc_ref, ts_ref,
-    gq_ref, gk_ref, gv_ref, first_ref, second_ref, gdecay_ref, gskip_ref,
-    send_x, send_g, in_x, in_g, back_x, back_g, conv_in, grad_in,
-    params, stage, stage_x, raw_ref, env_ref, hid_hi, hid_lo, cos_ref, spec_h, spec_x, spec_g, wide,
-    gather, rs_out, rs_in, plane_in, tp_in, fin,
-    send_sem, x_sem, g_sem, cx_sem, cg_sem, z_sem, rz_sem, y_sem, ry_sem, t_sem, f_sem,
-):
+def kernel(*refs):
+    inputs, results, refs = refs[:OPERANDS], refs[OPERANDS : OPERANDS + 7], refs[OPERANDS + 7 :]
+    held, refs = refs[:OPERANDS], refs[OPERANDS:]
+    outs, refs = refs[:7], refs[7:]
+    (
+        q_ref, k_ref, v_ref, go_ref, w1_ref, w2_ref, decay_ref, skip_ref,
+        f1x_ref, f1_ref, f2_ref, i1_ref, i2_ref, pb_ref, pt_ref, turns_ref,
+    ) = held
+    gq_ref, gk_ref, gv_ref, first_ref, second_ref, gdecay_ref, gskip_ref = outs
+    (
+        send_x, send_g, in_x, in_g, back_x, back_g, conv_in, grad_in,
+        params, stage, stage_x, raw_ref, env_ref, hid_hi, hid_lo, cos_ref, spec_h, spec_x, spec_g, wide,
+        z_in, gather, plane_in, tp_in,
+        send_sem, x_sem, g_sem, cx_sem, cg_sem, z_sem, y_sem, ry_sem, t_sem, load_sem, save_sem,
+    ) = refs
+    twc_ref, tws_ref, tc_ref, ts_ref = (turns_ref.at[i] for i in range(4))
+
+    def load(at):
+        return pltpu.make_async_copy(inputs[at], held[at], load_sem.at[at])
+
+    def save(at):
+        return pltpu.make_async_copy(outs[at], results[at], save_sem.at[at])
+
+    for at in (1, 2, 0, 3, *range(4, OPERANDS)):
+        load(at).start()
+
     me = lax.axis_index("seq")
     my_tp = lax.axis_index("tp")
     my_z, my_y = me // PLANE, me % PLANE
@@ -134,40 +149,42 @@
 
         lax.fori_loop(0, 4, step, 0)
 
-    def exchange(out_ref, in_ref, recv_sem, send_at):
+    def exchange(out_ref, in_ref, recv_sem, send_at, first, last):
+        def send(peer):
+            pltpu.make_async_remote_copy(
+                src_ref=out_ref.at[peer],
+                dst_ref=in_ref.at[me],
+                send_sem=send_sem.at[send_at],
+                recv_sem=recv_sem,
+                device_id={"seq": peer},
+                device_id_type=MESH,
+            ).start()
+
         def step(i, carry):
-            for peer in ((me + i) % SEQ, (me + SEQ - i) % SEQ):
-                pltpu.make_async_remote_copy(
-                    src_ref=out_ref.at[peer],
-                    dst_ref=in_ref.at[me],
-                    send_sem=send_sem.at[send_at],
-                    recv_sem=recv_sem,
-                    device_id={"seq": peer},
-                    device_id_type=MESH,
-                ).start()
-            return carry
-
-        lax.fori_loop(1, SEQ // 2, step, 0)
-        peer = (me + SEQ // 2) % SEQ
-        pltpu.make_async_remote_copy(
-            src_ref=out_ref.at[peer],
-            dst_ref=in_ref.at[me],
-            send_sem=send_sem.at[send_at],
-            recv_sem=recv_sem,
-            device_id={"seq": peer},
-            device_id_type=MESH,
-        ).start()
-        in_ref[me] = out_ref[me]
+            offset = (i * 11) % 32
+            send((me + offset) % SEQ)
+            send((me + SEQ - offset) % SEQ)
+            return carry
+
+        lax.fori_loop(max(first, 1), last, step, 0)
+        if first == 0:
+            send((me + SEQ // 2) % SEQ)
+            in_ref[me] = out_ref[me]
 
     def wait_bytes(ref, count, sem):
         view = ref.at[pl.ds(0, count)]
         pltpu.make_async_copy(view, view, sem).wait()
 
+    load(1).wait()
+    load(2).wait()
     gate(k_ref, v_ref, send_x)
+    load(0).wait()
+    load(3).wait()
+    gate(q_ref, go_ref, send_g)
     pl.semaphore_wait(barrier, SEQ - 1 + TP - 1)
-    exchange(send_x, in_x, x_sem, 0)
-    gate(q_ref, go_ref, send_g)
-    exchange(send_g, in_g, g_sem, 1)
+    exchange(send_x, in_x, x_sem, 0, 0, 32)
+    for at in range(4, OPERANDS):
+        load(at).wait()
 
     for half in range(2):
         lanes = pl.ds(pl.multiple_of(half * 512 + (me // 16) * B, B), B)
@@ -298,20 +315,17 @@
         lax.fori_loop(0, J // 8, step, 0)
 
     forward(stage, spec_h, False)
+    exchange(send_g, in_g, g_sem, 1, 0, 32)
     wait_bytes(in_x, SEQ - 1, x_sem)
     widen(in_x, stage_x)
     forward(stage_x, spec_x, True)
     inverse(spec_h, spec_x, False)
     finish(in_x, back_x)
-    exchange(back_x, conv_in, cx_sem, 2)
+    exchange(back_x, conv_in, cx_sem, 2, 0, 32)
 
     wait_bytes(in_g, SEQ - 1, g_sem)
     widen(in_g, stage)
     forward(stage, spec_g, True)
-    inverse(spec_h, spec_g, True)
-    finish(in_g, back_g)
-    exchange(back_g, grad_in, cg_sem, 3)
-
     inverse(spec_x, spec_g, True)
 
     def reduce_filter(at, carry):
@@ -358,7 +372,7 @@
     packed = jnp.transpose(wide[...])[:C]
     packed = jnp.where(lane == 64, -scale * jnp.sum(decay_sum, axis=1, keepdims=True), packed)
     packed = jnp.where(lane == 65, scale * jnp.sum(skip_sum, axis=1, keepdims=True), packed)
-    gather[my_z, my_y] = packed.astype(BF16)
+    z_in[my_z, 0] = packed.astype(BF16)
 
     lane_64 = lax.broadcasted_iota(jnp.int32, (64, B), 1)
     swapped = jnp.where(lane_64 < 16, pltpu.roll(sin_sum, B - 16, 1), pltpu.roll(sin_sum, 16, 1))
@@ -366,36 +380,42 @@
     wide[64:, :] = jnp.zeros((64, B), F32)
     first = jnp.transpose(wide[...])
     first = jnp.where(lane < 64, first[:16], pltpu.roll(first[16:32], 64, 1))
-    for i in range(DEPTH):
-        rs_out[i] = first[i : i + 1]
-    rs_in[my_z] = rs_out[my_z]
-
-    def send_z(i, carry):
-        peer = (my_z + i) % DEPTH
-        pltpu.make_async_remote_copy(
-            src_ref=rs_out.at[peer],
-            dst_ref=rs_in.at[my_z],
-            send_sem=send_sem.at[4],
-            recv_sem=rz_sem,
-            device_id={"seq": peer * PLANE + my_y},
-            device_id_type=MESH,
-        ).start()
-        pltpu.make_async_remote_copy(
-            src_ref=gather.at[my_z, my_y],
-            dst_ref=gather.at[my_z, my_y],
-            send_sem=send_sem.at[5],
-            recv_sem=z_sem,
-            device_id={"seq": peer * PLANE + my_y},
-            device_id_type=MESH,
-        ).start()
-        return carry
-
-    lax.fori_loop(1, DEPTH, send_z, 0)
+    z_in[my_z, 1] = first.astype(BF16)
+
+    def spread(ref, mine, sem, send_at, count, peer_of):
+        def step(i, carry):
+            pltpu.make_async_remote_copy(
+                src_ref=ref.at[mine],
+                dst_ref=ref.at[mine],
+                send_sem=send_sem.at[send_at],
+                recv_sem=sem,
+                device_id=peer_of((mine + i) % count),
+                device_id_type=MESH,
+            ).start()
+            return carry
+
+        lax.fori_loop(1, count, step, 0)
+
+    def on_plane(peer):
+        return {"seq": my_z * PLANE + peer}
+
+    spread(z_in, my_z, z_sem, 4, DEPTH, lambda peer: {"seq": peer * PLANE + my_y})
+    inverse(spec_h, spec_g, True)
+    finish(in_g, back_g)
+    exchange(back_g, grad_in, cg_sem, 3, 0, 32)
 
     def to_rows(in_ref, at, half):
         block = in_ref[pl.ds(at * 16, 16)].astype(F32)[:, half * 8 : (half + 1) * 8]
         return jnp.transpose(block.reshape(B, B))
 
+    wait_bytes(z_in, DEPTH - 1, z_sem)
+    total = z_in[0, 1].astype(F32)
+    for i in range(1, DEPTH):
+        total += z_in[i, 1].astype(F32)
+    plane_in[my_y] = total
+    spread(plane_in, my_y, ry_sem, 6, PLANE, on_plane)
+    gather[my_y] = z_in[:, 0]
+    spread(gather, my_y, y_sem, 5, PLANE, on_plane)
     wait_bytes(conv_in, SEQ - 1, cx_sem)
 
     def rows_q(at, carry):
@@ -406,77 +426,38 @@
 
     lax.fori_loop(0, 4, rows_q, 0)
 
-    wait_bytes(rs_in, DEPTH - 1, rz_sem)
-    total = rs_in[0]
-    for i in range(1, DEPTH):
-        total += rs_in[i]
-    plane_in[my_y] = total
-
-    def send_plane(i, carry):
-        peer = (my_y + i) % PLANE
-        pltpu.make_async_remote_copy(
-            src_ref=plane_in.at[my_y],
-            dst_ref=plane_in.at[my_y],
-            send_sem=send_sem.at[6],
-            recv_sem=ry_sem,
-            device_id={"seq": my_z * PLANE + peer},
-            device_id_type=MESH,
-        ).start()
-        return carry
-
-    lax.fori_loop(1, PLANE, send_plane, 0)
-    wait_bytes(gather.at[:, 0], DEPTH - 1, z_sem)
-
-    def send_gather(i, carry):
-        peer = (my_y + i) % PLANE
-        pltpu.make_async_remote_copy(
-            src_ref=gather.at[:, my_y],
-            dst_ref=gather.at[:, my_y],
-            send_sem=send_sem.at[7],
-            recv_sem=y_sem,
-            device_id={"seq": my_z * PLANE + peer},
-            device_id_type=MESH,
-        ).start()
-        return carry
-
-    lax.fori_loop(1, PLANE, send_gather, 0)
+    save(0).start()
     wait_bytes(plane_in, PLANE - 1, ry_sem)
     total = plane_in[0]
     for i in range(1, PLANE):
         total += plane_in[i]
     tp_in[my_tp] = total
-
-    def send_tp(i, carry):
-        pltpu.make_async_remote_copy(
-            src_ref=tp_in.at[my_tp],
-            dst_ref=tp_in.at[my_tp],
-            send_sem=send_sem.at[8],
-            recv_sem=t_sem,
-            device_id={"tp": (my_tp + i) % TP},
-            device_id_type=MESH,
-        ).start()
+    spread(tp_in, my_tp, t_sem, 7, TP, lambda peer: {"tp": peer})
+    wait_bytes(gather, PLANE - 1, y_sem)
+
+    def columns(at, carry):
+        for half in range(2):
+            lanes = pl.ds(pl.multiple_of(half * 512 + at * B, B), B)
+            parts = [
+                gather[y, at * 4 + z].astype(F32)[half * 8 : (half + 1) * 8]
+                for z in range(4)
+                for y in range(PLANE)
+            ]
+            turned = jnp.transpose(jnp.concatenate(parts, axis=0))
+            second_ref[:, lanes] = turned[:64]
+            gdecay_ref[:, lanes] = turned[64:65]
+            gskip_ref[:, lanes] = turned[65:66]
         return carry
 
-    lax.fori_loop(1, TP, send_tp, 0)
+    lax.fori_loop(0, 4, columns, 0)
     wait_bytes(tp_in, TP - 1, t_sem)
     total = tp_in[0]
     for i in range(1, TP):
         total += tp_in[i]
-    fin[my_z] = total
-
-    def send_fin(i, carry):
-        peer = (my_z + i) % DEPTH
-        pltpu.make_async_remote_copy(
-            src_ref=fin.at[my_z],
-            dst_ref=fin.at[my_z],
-            send_sem=send_sem.at[9],
-            recv_sem=f_sem,
-            device_id={"seq": peer * PLANE + my_y},
-            device_id_type=MESH,
-        ).start()
-        return carry
-
-    lax.fori_loop(1, DEPTH, send_fin, 0)
+    first_ref[:16, :] = total[:, :64]
+    first_ref[16:, :] = pltpu.roll(total, 64, 1)[:, :64]
+    for at in range(3, 7):
+        save(at).start()
 
     wait_bytes(grad_in, SEQ - 1, cg_sem)
 
@@ -489,37 +470,30 @@
         return carry
 
     lax.fori_loop(0, 4, rows_kv, 0)
-
-    others = gather.at[:, pl.ds(0, PLANE - 1)]
-    pltpu.make_async_copy(others, others, y_sem).wait()
-
-    def columns(at, carry):
-        for half in range(2):
-            lanes = pl.ds(pl.multiple_of(half * 512 + at * B, B), B)
-            block = gather[pl.ds(at * 4, 4)].astype(F32).reshape(16, C, B)[:, half * 8 : (half + 1) * 8]
-            turned = jnp.transpose(block.reshape(B, B))
-            second_ref[:, lanes] = turned[:64]
-            gdecay_ref[:, lanes] = turned[64:65]
-            gskip_ref[:, lanes] = turned[65:66]
-        return carry
-
-    lax.fori_loop(0, 4, columns, 0)
-
-    wait_bytes(fin, DEPTH - 1, f_sem)
-    for i in range(DEPTH):
-        wide[i : i + 1, :] = fin[i]
-    total = wide[:DEPTH, :]
-    first_ref[:16, :] = total[:, :64]
-    first_ref[16:, :] = pltpu.roll(total, 64, 1)[:, :64]
+    save(1).start()
+    save(2).start()
 
     for at, ref in enumerate((send_x, send_g, back_x, back_g)):
         wait_bytes(ref, SEQ - 1, send_sem.at[at])
-    wait_bytes(rs_out, DEPTH - 1, send_sem.at[4])
-    wait_bytes(gather.at[:, 0], DEPTH - 1, send_sem.at[5])
+    wait_bytes(z_in, DEPTH - 1, send_sem.at[4])
+    wait_bytes(gather, PLANE - 1, send_sem.at[5])
     wait_bytes(plane_in, PLANE - 1, send_sem.at[6])
-    pltpu.make_async_copy(others, others, send_sem.at[7]).wait()
-    wait_bytes(tp_in, TP - 1, send_sem.at[8])
-    wait_bytes(fin, DEPTH - 1, send_sem.at[9])
+    wait_bytes(tp_in, TP - 1, send_sem.at[7])
+    for at in range(7):
+        save(at).wait()
+
+
+def copy_kernel(*refs):
+    sources, targets, held, load_sem, save_sem = refs[:7], refs[7:14], refs[14:21], refs[21], refs[22]
+    loads = [pltpu.make_async_copy(sources[i], held[i], load_sem.at[i]) for i in range(7)]
+    saves = [pltpu.make_async_copy(held[i], targets[i], save_sem.at[i]) for i in range(7)]
+    for copy in loads:
+        copy.start()
+    for load, copy in zip(loads, saves):
+        load.wait()
+        copy.start()
+    for copy in saves:
+        copy.wait()
 
 
 def per_device(q_proj, k_proj, v_proj, grad_out, w_first, w_second, decay_rate, skip_gain):
@@ -530,38 +504,49 @@
     full = pltpu.VMEM((J * C, B), F32)
     spectrum = pltpu.VMEM((C * J, 2 * B), F32)
     dma = pltpu.SemaphoreType.DMA
-    vmem = pl.BlockSpec(memory_space=pltpu.VMEM)
-    grad_q, grad_k, grad_v, first, second, decay, skip = pl.pallas_call(
+    anywhere = pl.BlockSpec(memory_space=pl.ANY)
+    operands = (
+        q_proj, k_proj, v_proj, grad_out, w_first, w_second,
+        decay_rate.reshape(1, chan), skip_gain.reshape(1, chan), *tables,
+    )
+    shapes = (
+        rows,
+        rows,
+        rows,
+        jax.ShapeDtypeStruct(w_first.shape, F32),
+        jax.ShapeDtypeStruct(w_second.shape, F32),
+        jax.ShapeDtypeStruct((1, chan), F32),
+        jax.ShapeDtypeStruct((1, chan), F32),
+    )
+    results = pl.pallas_call(
         kernel,
-        out_shape=(
-            rows,
-            rows,
-            rows,
-            jax.ShapeDtypeStruct(w_first.shape, F32),
-            jax.ShapeDtypeStruct(w_second.shape, F32),
-            jax.ShapeDtypeStruct((1, chan), F32),
-            jax.ShapeDtypeStruct((1, chan), F32),
-        ),
-        in_specs=[vmem] * (8 + len(tables)),
-        out_specs=[vmem] * 7,
-        scratch_shapes=[block] * 8
+        out_shape=shapes,
+        in_specs=[anywhere] * OPERANDS,
+        out_specs=[anywhere] * 7,
+        scratch_shapes=[pltpu.VMEM(x.shape, x.dtype) for x in (*operands, *shapes)]
+        + [block] * 8
         + [pltpu.VMEM((2, B, B), F32)]
         + [full] * 4
         + [pltpu.VMEM((J * 64, B), BF16)] * 2
         + [pltpu.VMEM((J * 64, B), F32)]
         + [spectrum] * 3
         + [pltpu.VMEM((B, B), F32)]
-        + [pltpu.VMEM((DEPTH, PLANE, C, B), BF16)]
-        + [pltpu.VMEM((count, 1, B), F32) for count in (DEPTH, DEPTH, PLANE, TP, DEPTH)]
-        + [dma((10,))]
-        + [dma(())] * 10,
+        + [pltpu.VMEM((DEPTH, 2, C, B), BF16), pltpu.VMEM((PLANE, DEPTH, C, B), BF16)]
+        + [pltpu.VMEM((count, C, B), F32) for count in (PLANE, TP)]
+        + [dma((8,))]
+        + [dma(())] * 8
+        + [dma((OPERANDS,)), dma((7,))],
         compiler_params=pltpu.CompilerParams(
-            collective_id=0, has_side_effects=True, vmem_limit_bytes=48 * 1024 * 1024
+            collective_id=0, has_side_effects=True, vmem_limit_bytes=56 * 1024 * 1024
         ),
-    )(
-        q_proj, k_proj, v_proj, grad_out, w_first, w_second,
-        decay_rate.reshape(1, chan), skip_gain.reshape(1, chan), *tables,
-    )
+    )(*operands)
+    grad_q, grad_k, grad_v, first, second, decay, skip = pl.pallas_call(
+        copy_kernel,
+        out_shape=shapes,
+        in_specs=[anywhere] * 7,
+        out_specs=[anywhere] * 7,
+        scratch_shapes=[pltpu.VMEM(x.shape, x.dtype) for x in shapes] + [dma((7,))] * 2,
+    )(*results)
     return grad_q, grad_k, grad_v, first, second, decay.reshape(chan), skip.reshape(chan)
 
 

time: 108 us -> 84 us (0.78)
  the two profiles are of different devices: /device:TPU:16 before, /device:TPU:1 now
where the time goes in v2:
time: 84 us; the launch traced here: 83.8 us
  Pallas kernels  83.2 us (99%)
    pallas_call x1, Pallas kernels, per_device(): pl.pallas_call(kernel, out_shape=shapes, in_specs=[anywhere] * OPERANDS,...  81.2 us
    pallas_call x1, Pallas kernels, per_device(): pl.pallas_call(copy_kernel, out_shape=shapes, in_specs=[anywhere] * 7, ou...  2.04 us

profile of v2, /device:TPU:1, one launch (start us, length us, event | category | flops | bytes accessed | tf_op | source)
XLA Modules:
  0.0 83.8 jit_solution(4872800369457337550)
XLA Ops:
  0.6 81.2 %shard_map.207 = (bf16[128,1024]{1,0:T(8,128)(2,1)}, bf16[128,1024]{1,0:T(8,128)(2,1)}, bf16[128,1024]{1,0:T(8,128)(2,1)}, f32[32,64]{1,0:T(8,128)}, f32[64,1024...) custom-call(bf16[128,1024]{1,0:T(8,128)(2,1)} %refs_0_.1, bf16[128,1024]{1,0:T(8,128)(2,1)} %refs_1_.1, ...), custom_call_target="tpu_custom_call" | custom-call | tf_op jit(solution)/shard_map/pallas_call | solution.py:521
  81.8 2.0 %shard_map.208 = (bf16[128,1024]{1,0:T(8,128)(2,1)}, bf16[128,1024]{1,0:T(8,128)(2,1)}, bf16[128,1024]{1,0:T(8,128)(2,1)}, f32[32,64]{1,0:T(8,128)}, f32[64,1024...) custom-call(bf16[128,1024]{1,0:T(8,128)(2,1)} %get-tuple-element.21.refs_0_, ...), custom_call_target="tpu_custom_call" | custom-call | tf_op jit(solution)/shard_map/pallas_call | solution.py:543

commit v3 on v2

--- a/solution.py
+++ b/solution.py
@@ -16,7 +16,9 @@
 B = 128
 C = 16
 L = J * B
-GROUP = 4
+GROUP = 16
+NET = 16
+RED = 16
 SEQ = 64
 TP = 8
 OPERANDS = 16
@@ -89,9 +91,8 @@
 
 
 def kernel(*refs):
-    inputs, results, refs = refs[:OPERANDS], refs[OPERANDS : OPERANDS + 7], refs[OPERANDS + 7 :]
+    inputs, outs, refs = refs[:OPERANDS], refs[OPERANDS : OPERANDS + 7], refs[OPERANDS + 7 :]
     held, refs = refs[:OPERANDS], refs[OPERANDS:]
-    outs, refs = refs[:7], refs[7:]
     (
         q_ref, k_ref, v_ref, go_ref, w1_ref, w2_ref, decay_ref, skip_ref,
         f1x_ref, f1_ref, f2_ref, i1_ref, i2_ref, pb_ref, pt_ref, turns_ref,
@@ -100,16 +101,13 @@
     (
         send_x, send_g, in_x, in_g, back_x, back_g, conv_in, grad_in,
         params, stage, stage_x, raw_ref, env_ref, hid_hi, hid_lo, cos_ref, spec_h, spec_x, spec_g, wide,
-        z_in, gather, plane_in, tp_in,
-        send_sem, x_sem, g_sem, cx_sem, cg_sem, z_sem, y_sem, ry_sem, t_sem, load_sem, save_sem,
+        z_in, gather, rs_out, rs_in, plane_in, tp_in, fin,
+        send_sem, x_sem, g_sem, cx_sem, cg_sem, z_sem, rz_sem, y_sem, ry_sem, t_sem, f_sem, load_sem,
     ) = refs
     twc_ref, tws_ref, tc_ref, ts_ref = (turns_ref.at[i] for i in range(4))
 
     def load(at):
         return pltpu.make_async_copy(inputs[at], held[at], load_sem.at[at])
-
-    def save(at):
-        return pltpu.make_async_copy(outs[at], results[at], save_sem.at[at])
 
     for at in (1, 2, 0, 3, *range(4, OPERANDS)):
         load(at).start()
@@ -178,11 +176,11 @@
     load(1).wait()
     load(2).wait()
     gate(k_ref, v_ref, send_x)
+    pl.semaphore_wait(barrier, SEQ - 1 + TP - 1)
+    exchange(send_x, in_x, x_sem, 0, 0, 32)
     load(0).wait()
     load(3).wait()
     gate(q_ref, go_ref, send_g)
-    pl.semaphore_wait(barrier, SEQ - 1 + TP - 1)
-    exchange(send_x, in_x, x_sem, 0, 0, 32)
     for at in range(4, OPERANDS):
         load(at).wait()
 
@@ -216,29 +214,29 @@
     turned = jnp.transpose(wide[...])[:64]
     wide[:, :64] = jnp.concatenate([w_swap] * 4, axis=0)
     turned_swap = jnp.transpose(wide[...])[:64]
-    lane_b = lax.broadcasted_iota(jnp.int32, (GROUP * 64, B), 1)
+    lane_b = lax.broadcasted_iota(jnp.int32, (NET * 64, B), 1)
     position = lax.broadcasted_iota(jnp.int32, (C, B), 1).astype(F32)
 
     def network(at, carry):
         pieces = []
-        for i in range(GROUP):
-            j = at * GROUP + i
+        for i in range(NET):
+            j = at * NET + i
             pieces.append(turned * tc_ref[pl.ds(j, 1), :] + turned_swap * ts_ref[pl.ds(j, 1), :])
         values = jnp.concatenate(pieces, axis=0)
         high = values.astype(BF16).astype(F32)
         left = jnp.where(lane_b < 64, high, values - high).astype(BF16)
         sine, cosine = sin_cos(dot(left, pb_ref[...]))
-        rows = pl.ds(pl.multiple_of(at * GROUP * 64, GROUP * 64), GROUP * 64)
+        rows = pl.ds(pl.multiple_of(at * NET * 64, NET * 64), NET * 64)
         cos_ref[rows, :] = cosine
         high, low = split(sine)
         hid_hi[rows, :] = high
         hid_lo[rows, :] = low
-        for i in range(0, GROUP, 2):
+        for i in range(0, NET, 2):
             h = jnp.concatenate([high[i * 64 : (i + 1) * 64], high[(i + 1) * 64 : (i + 2) * 64]], axis=1)
             l = jnp.concatenate([low[i * 64 : (i + 1) * 64], low[(i + 1) * 64 : (i + 2) * 64]], axis=1)
             raw = dot(w_rows, jnp.concatenate([h, h, l, l], axis=0))
             for o in range(2):
-                j = at * GROUP + i + o
+                j = at * NET + i + o
                 fraction = (position + (j * B).astype(F32)) * (1.0 / L)
                 envelope = jnp.exp(-decay * fraction) * scale
                 part = raw[:, o * B : (o + 1) * B]
@@ -248,7 +246,7 @@
                 stage[here, :] = part * envelope
         return carry
 
-    lax.fori_loop(0, J // GROUP, network, 0)
+    lax.fori_loop(0, J // NET, network, 0)
 
     def forward(from_ref, spec_ref, exact):
         def step(at, carry):
@@ -326,13 +324,16 @@
     wait_bytes(in_g, SEQ - 1, g_sem)
     widen(in_g, stage)
     forward(stage, spec_g, True)
+    inverse(spec_h, spec_g, True)
+    finish(in_g, back_g)
+    exchange(back_g, grad_in, cg_sem, 3, 0, 4)
     inverse(spec_x, spec_g, True)
 
     def reduce_filter(at, carry):
         decay_sum, skip_sum, second, cos_sum, sin_sum = carry
         left, right, hid_rows = [], [], []
-        for i in range(GROUP):
-            j = at * GROUP + i
+        for i in range(RED):
+            j = at * RED + i
             here = pl.ds(pl.multiple_of(j * C, C), C)
             grad_raw = stage[here, :] * env_ref[here, :]
             fraction = (position + (j * B).astype(F32)) * (1.0 / L)
@@ -350,11 +351,11 @@
             (((1,), (1,)), ((), ())),
             preferred_element_type=F32,
         )
-        rows = pl.ds(pl.multiple_of(at * GROUP * 64, GROUP * 64), GROUP * 64)
+        rows = pl.ds(pl.multiple_of(at * RED * 64, RED * 64), RED * 64)
         high, low = split(jnp.concatenate(left, axis=0) * cos_ref[rows, :])
         turned = dot(jnp.concatenate([high, low, high], axis=1), pt_ref[...])
-        for i in range(GROUP):
-            j = at * GROUP + i
+        for i in range(RED):
+            j = at * RED + i
             part = turned[i * 64 : (i + 1) * 64]
             cos_sum += part * tc_ref[pl.ds(j, 1), :]
             sin_sum += part * ts_ref[pl.ds(j, 1), :]
@@ -363,16 +364,18 @@
     zero = jnp.zeros((C, B), F32)
     decay_sum, skip_sum, second, cos_sum, sin_sum = lax.fori_loop(
         0,
-        J // GROUP,
+        J // RED,
         reduce_filter,
         (zero, zero, jnp.zeros((64, C), F32), jnp.zeros((64, B), F32), jnp.zeros((64, B), F32)),
     )
     wide[...] = jnp.zeros((B, B), F32)
     wide[:64, :C] = second * scale
     packed = jnp.transpose(wide[...])[:C]
-    packed = jnp.where(lane == 64, -scale * jnp.sum(decay_sum, axis=1, keepdims=True), packed)
-    packed = jnp.where(lane == 65, scale * jnp.sum(skip_sum, axis=1, keepdims=True), packed)
-    z_in[my_z, 0] = packed.astype(BF16)
+    packed = jnp.where(lane[:8] < 64, packed[:8], pltpu.roll(packed[8:], 64, 1))
+    row = lax.broadcasted_iota(jnp.int32, (C, B), 0)
+    sums = jnp.where(lane == row, -scale * jnp.sum(decay_sum, axis=1, keepdims=True), 0.0)
+    sums += jnp.where(lane == row + C, scale * jnp.sum(skip_sum, axis=1, keepdims=True), 0.0)
+    sums = jnp.sum(sums, axis=0, keepdims=True)
 
     lane_64 = lax.broadcasted_iota(jnp.int32, (64, B), 1)
     swapped = jnp.where(lane_64 < 16, pltpu.roll(sin_sum, B - 16, 1), pltpu.roll(sin_sum, 16, 1))
@@ -380,16 +383,23 @@
     wide[64:, :] = jnp.zeros((64, B), F32)
     first = jnp.transpose(wide[...])
     first = jnp.where(lane < 64, first[:16], pltpu.roll(first[16:32], 64, 1))
-    z_in[my_z, 1] = first.astype(BF16)
-
-    def spread(ref, mine, sem, send_at, count, peer_of):
+    for i in range(DEPTH):
+        rs_out[i] = first[i : i + 1]
+    rs_in[my_z] = rs_out[my_z]
+    wide[:8, :] = packed
+    wide[8:9, :] = sums
+    wide[9:16, :] = jnp.zeros((7, B), F32)
+    z_in[my_z] = wide[:C, :].astype(BF16)
+
+    def spread(ref, mine, sem, send_at, count, peer_of, parts=None):
         def step(i, carry):
+            peer = (mine + i) % count
             pltpu.make_async_remote_copy(
-                src_ref=ref.at[mine],
+                src_ref=ref.at[mine] if parts is None else parts.at[peer],
                 dst_ref=ref.at[mine],
                 send_sem=send_sem.at[send_at],
                 recv_sem=sem,
-                device_id=peer_of((mine + i) % count),
+                device_id=peer_of(peer),
                 device_id_type=MESH,
             ).start()
             return carry
@@ -399,23 +409,32 @@
     def on_plane(peer):
         return {"seq": my_z * PLANE + peer}
 
-    spread(z_in, my_z, z_sem, 4, DEPTH, lambda peer: {"seq": peer * PLANE + my_y})
-    inverse(spec_h, spec_g, True)
-    finish(in_g, back_g)
-    exchange(back_g, grad_in, cg_sem, 3, 0, 32)
+    def on_depth(peer):
+        return {"seq": peer * PLANE + my_y}
+
+    spread(rs_in, my_z, rz_sem, 4, DEPTH, on_depth, rs_out)
+    spread(z_in, my_z, z_sem, 5, DEPTH, on_depth)
+    exchange(back_g, grad_in, cg_sem, 3, 4, 32)
 
     def to_rows(in_ref, at, half):
         block = in_ref[pl.ds(at * 16, 16)].astype(F32)[:, half * 8 : (half + 1) * 8]
         return jnp.transpose(block.reshape(B, B))
 
+    def add(ref, count):
+        total = ref[0]
+        for i in range(1, count):
+            total += ref[i]
+        return total
+
+    wait_bytes(rs_in, DEPTH - 1, rz_sem)
+    plane_in[my_y] = add(rs_in, DEPTH)
+    spread(plane_in, my_y, ry_sem, 6, PLANE, on_plane)
     wait_bytes(z_in, DEPTH - 1, z_sem)
-    total = z_in[0, 1].astype(F32)
-    for i in range(1, DEPTH):
-        total += z_in[i, 1].astype(F32)
-    plane_in[my_y] = total
-    spread(plane_in, my_y, ry_sem, 6, PLANE, on_plane)
-    gather[my_y] = z_in[:, 0]
-    spread(gather, my_y, y_sem, 5, PLANE, on_plane)
+    gather[my_y] = z_in[...]
+    spread(gather, my_y, y_sem, 7, PLANE, on_plane)
+    wait_bytes(plane_in, PLANE - 1, ry_sem)
+    tp_in[my_tp] = add(plane_in, PLANE)
+    spread(tp_in, my_tp, t_sem, 8, TP, lambda peer: {"tp": peer})
     wait_bytes(conv_in, SEQ - 1, cx_sem)
 
     def rows_q(at, carry):
@@ -426,38 +445,31 @@
 
     lax.fori_loop(0, 4, rows_q, 0)
 
-    save(0).start()
-    wait_bytes(plane_in, PLANE - 1, ry_sem)
-    total = plane_in[0]
-    for i in range(1, PLANE):
-        total += plane_in[i]
-    tp_in[my_tp] = total
-    spread(tp_in, my_tp, t_sem, 7, TP, lambda peer: {"tp": peer})
+    wait_bytes(tp_in, TP - 1, t_sem)
+    fin[my_z] = add(tp_in, TP)
+    spread(fin, my_z, f_sem, 9, DEPTH, on_depth)
     wait_bytes(gather, PLANE - 1, y_sem)
 
+    source = lax.broadcasted_iota(jnp.int32, (B, 4 * B), 0)
+    target = lax.broadcasted_iota(jnp.int32, (B, 4 * B), 1)
+    pick = jnp.where(source == target // B * 8 + target % 8, 1.0, 0.0).astype(BF16)
+    own = lane // 8 == lax.broadcasted_iota(jnp.int32, (C, B), 0)
+
     def columns(at, carry):
+        tiles = [gather[y, at * 4 + z].astype(F32) for z in range(4) for y in range(PLANE)]
+        turned = jnp.transpose(jnp.concatenate([tile[:8] for tile in tiles], axis=0))
+        for i, tile in enumerate(tiles):
+            wide[i : i + 1, :] = tile[8:9]
+        rows = dot(wide[:C, :].astype(BF16), pick)
         for half in range(2):
             lanes = pl.ds(pl.multiple_of(half * 512 + at * B, B), B)
-            parts = [
-                gather[y, at * 4 + z].astype(F32)[half * 8 : (half + 1) * 8]
-                for z in range(4)
-                for y in range(PLANE)
-            ]
-            turned = jnp.transpose(jnp.concatenate(parts, axis=0))
-            second_ref[:, lanes] = turned[:64]
-            gdecay_ref[:, lanes] = turned[64:65]
-            gskip_ref[:, lanes] = turned[65:66]
+            second_ref[:, lanes] = turned[half * 64 : (half + 1) * 64]
+            for ref, q in ((gdecay_ref, half), (gskip_ref, 2 + half)):
+                part = jnp.where(own, rows[:, q * B : (q + 1) * B], 0.0)
+                ref[:, lanes] = jnp.sum(part, axis=0, keepdims=True)
         return carry
 
     lax.fori_loop(0, 4, columns, 0)
-    wait_bytes(tp_in, TP - 1, t_sem)
-    total = tp_in[0]
-    for i in range(1, TP):
-        total += tp_in[i]
-    first_ref[:16, :] = total[:, :64]
-    first_ref[16:, :] = pltpu.roll(total, 64, 1)[:, :64]
-    for at in range(3, 7):
-        save(at).start()
 
     wait_bytes(grad_in, SEQ - 1, cg_sem)
 
@@ -470,29 +482,29 @@
         return carry
 
     lax.fori_loop(0, 4, rows_kv, 0)
-    save(1).start()
-    save(2).start()
+
+    wait_bytes(fin, DEPTH - 1, f_sem)
+    for i in range(DEPTH):
+        wide[i : i + 1, :] = fin[i]
+    total = wide[:C, :]
+    first_ref[:16, :] = total[:, :64]
+    first_ref[16:, :] = pltpu.roll(total, 64, 1)[:, :64]
 
     for at, ref in enumerate((send_x, send_g, back_x, back_g)):
         wait_bytes(ref, SEQ - 1, send_sem.at[at])
-    wait_bytes(z_in, DEPTH - 1, send_sem.at[4])
-    wait_bytes(gather, PLANE - 1, send_sem.at[5])
+    wait_bytes(rs_out, DEPTH - 1, send_sem.at[4])
+    wait_bytes(z_in, DEPTH - 1, send_sem.at[5])
     wait_bytes(plane_in, PLANE - 1, send_sem.at[6])
-    wait_bytes(tp_in, TP - 1, send_sem.at[7])
-    for at in range(7):
-        save(at).wait()
+    wait_bytes(gather, PLANE - 1, send_sem.at[7])
+    wait_bytes(tp_in, TP - 1, send_sem.at[8])
+    wait_bytes(fin, DEPTH - 1, send_sem.at[9])
 
 
 def copy_kernel(*refs):
-    sources, targets, held, load_sem, save_sem = refs[:7], refs[7:14], refs[14:21], refs[21], refs[22]
-    loads = [pltpu.make_async_copy(sources[i], held[i], load_sem.at[i]) for i in range(7)]
-    saves = [pltpu.make_async_copy(held[i], targets[i], save_sem.at[i]) for i in range(7)]
-    for copy in loads:
+    copies = [pltpu.make_async_copy(refs[i], refs[7 + i], refs[14].at[i]) for i in range(7)]
+    for copy in copies:
         copy.start()
-    for load, copy in zip(loads, saves):
-        load.wait()
-        copy.start()
-    for copy in saves:
+    for copy in copies:
         copy.wait()
 
 
@@ -505,6 +517,7 @@
     spectrum = pltpu.VMEM((C * J, 2 * B), F32)
     dma = pltpu.SemaphoreType.DMA
     anywhere = pl.BlockSpec(memory_space=pl.ANY)
+    vmem = pl.BlockSpec(memory_space=pltpu.VMEM)
     operands = (
         q_proj, k_proj, v_proj, grad_out, w_first, w_second,
         decay_rate.reshape(1, chan), skip_gain.reshape(1, chan), *tables,
@@ -520,10 +533,10 @@
     )
     results = pl.pallas_call(
         kernel,
-        out_shape=shapes,
+        out_shape=[pltpu.VMEM(x.shape, x.dtype) for x in shapes],
         in_specs=[anywhere] * OPERANDS,
-        out_specs=[anywhere] * 7,
-        scratch_shapes=[pltpu.VMEM(x.shape, x.dtype) for x in (*operands, *shapes)]
+        out_specs=[vmem] * 7,
+        scratch_shapes=[pltpu.VMEM(x.shape, x.dtype) for x in operands]
         + [block] * 8
         + [pltpu.VMEM((2, B, B), F32)]
         + [full] * 4
@@ -531,21 +544,22 @@
         + [pltpu.VMEM((J * 64, B), F32)]
         + [spectrum] * 3
         + [pltpu.VMEM((B, B), F32)]
-        + [pltpu.VMEM((DEPTH, 2, C, B), BF16), pltpu.VMEM((PLANE, DEPTH, C, B), BF16)]
-        + [pltpu.VMEM((count, C, B), F32) for count in (PLANE, TP)]
-        + [dma((8,))]
-        + [dma(())] * 8
-        + [dma((OPERANDS,)), dma((7,))],
+        + [pltpu.VMEM((DEPTH, C, B), BF16), pltpu.VMEM((PLANE, DEPTH, C, B), BF16)]
+        + [pltpu.VMEM((count, 1, B), F32) for count in (DEPTH, DEPTH, PLANE, TP, DEPTH)]
+        + [dma((10,))]
+        + [dma(())] * 10
+        + [dma((OPERANDS,))],
         compiler_params=pltpu.CompilerParams(
             collective_id=0, has_side_effects=True, vmem_limit_bytes=56 * 1024 * 1024
         ),
     )(*operands)
+    results = [pltpu.with_memory_space_constraint(x, pltpu.VMEM) for x in results]
     grad_q, grad_k, grad_v, first, second, decay, skip = pl.pallas_call(
         copy_kernel,
         out_shape=shapes,
-        in_specs=[anywhere] * 7,
+        in_specs=[vmem] * 7,
         out_specs=[anywhere] * 7,
-        scratch_shapes=[pltpu.VMEM(x.shape, x.dtype) for x in shapes] + [dma((7,))] * 2,
+        scratch_shapes=[dma((7,))],
     )(*results)
     return grad_q, grad_k, grad_v, first, second, decay.reshape(chan), skip.reshape(chan)
 

time: 84 us -> 76.9 us (0.915)
  Pallas kernels: 83.2 us -> 75.5 us
    pallas_call x2, Pallas kernels: 83.2 us -> 75.5 us  [the longest x1 74.5 us: per_device(): pl.pallas_call(kernel, out_shape=[pltpu.VMEM(x.shape, x.dtype) for x in s...]
where the time goes in v3:
time: 76.9 us; the launch traced here: 76.2 us
  Pallas kernels  75.5 us (98%)
    pallas_call x1, Pallas kernels, per_device(): pl.pallas_call(kernel, out_shape=[pltpu.VMEM(x.shape, x.dtype) for x in s...  74.5 us

profile of v3, /device:TPU:1, one launch (start us, length us, event | category | flops | bytes accessed | tf_op | source)
XLA Modules:
  0.0 76.2 jit_solution(11604656117570908343)
XLA Ops:
  0.6 74.5 %shard_map.207 = (bf16[128,1024]{1,0:T(8,128)(2,1)S(1)}, bf16[128,1024]{1,0:T(8,128)(2,1)S(1)}, bf16[128,1024]{1,0:T(8,128)(2,1)S(1)}, f32[32,64]{1,0:T(8,128)S(...) custom-call(bf16[128,1024]{1,0:T(8,128)(2,1)} %refs_0_.1, bf16[128,1024]{1,0:T(8,128)(2,1)} %refs_1_.1, ...), custom_call_target="tpu_custom_call" | custom-call | tf_op jit(solution)/shard_map/pallas_call | solution.py:534
  75.1 1.0 %shard_map.208 = (bf16[128,1024]{1,0:T(8,128)(2,1)}, bf16[128,1024]{1,0:T(8,128)(2,1)}, bf16[128,1024]{1,0:T(8,128)(2,1)}, f32[32,64]{1,0:T(8,128)}, f32[64,1024...) custom-call(bf16[128,1024]{1,0:T(8,128)(2,1)S(1)} %get-tuple-element.21.refs_0_, ...), custom_call_target="tpu_custom_call" | custom-call | tf_op jit(solution)/shard_map/pallas_call | solution.py:557

commit v4 on v3

--- a/solution.py
+++ b/solution.py
@@ -18,7 +18,7 @@
 L = J * B
 GROUP = 16
 NET = 16
-RED = 16
+RED = 32
 SEQ = 64
 TP = 8
 OPERANDS = 16
@@ -48,9 +48,8 @@
     inner = turn * (freq[:, None] * np.arange(B)[None, :] % L) / L
     p_high, p_low = split_np(np.concatenate([np.sin(inner), np.cos(inner)], axis=0))
     outer = turn * (np.arange(J)[:, None] * freq[None, :] % J) / J
-    pos_t = np.zeros((3 * B, B), np.float32).astype(jnp.bfloat16)
-    for at, part in enumerate((p_high, p_high, p_low)):
-        pos_t[at * B : (at + 1) * B, :32] = part.T
+    pos_t = np.zeros((2 * B, B), np.float32).astype(jnp.bfloat16)
+    pos_t[:B, :32], pos_t[:B, 32:64], pos_t[B:, :32] = p_high.T, p_low.T, p_high.T
     turn_cos = np.tile(np.concatenate([np.cos(outer), np.cos(outer)], axis=1), (1, 4))
     turn_sin = np.tile(np.concatenate([-np.sin(outer), np.sin(outer)], axis=1), (1, 4))
     return (
@@ -109,8 +108,8 @@
     def load(at):
         return pltpu.make_async_copy(inputs[at], held[at], load_sem.at[at])
 
-    for at in (1, 2, 0, 3, *range(4, OPERANDS)):
-        load(at).start()
+    load(1).start()
+    load(2).start()
 
     me = lax.axis_index("seq")
     my_tp = lax.axis_index("tp")
@@ -134,6 +133,9 @@
         return carry
 
     lax.fori_loop(1, TP, greet_tp, 0)
+
+    for at in (0, *range(3, OPERANDS)):
+        load(at).start()
 
     def gate(left_ref, right_ref, out_ref):
         def step(at, carry):
@@ -324,27 +326,26 @@
     wait_bytes(in_g, SEQ - 1, g_sem)
     widen(in_g, stage)
     forward(stage, spec_g, True)
-    inverse(spec_h, spec_g, True)
-    finish(in_g, back_g)
-    exchange(back_g, grad_in, cg_sem, 3, 0, 4)
     inverse(spec_x, spec_g, True)
 
     def reduce_filter(at, carry):
         decay_sum, skip_sum, second, cos_sum, sin_sum = carry
         left, right, hid_rows = [], [], []
-        for i in range(RED):
-            j = at * RED + i
-            here = pl.ds(pl.multiple_of(j * C, C), C)
-            grad_raw = stage[here, :] * env_ref[here, :]
-            fraction = (position + (j * B).astype(F32)) * (1.0 / L)
-            decay_sum += grad_raw * raw_ref[here, :] * fraction
-            skip_sum += in_x[j].astype(F32) * in_g[j].astype(F32)
-            high, low = split(grad_raw)
-            right.append(jnp.concatenate([high, high, low], axis=1))
-            rows = pl.ds(pl.multiple_of(j * 64, 64), 64)
-            h = hid_hi[rows, :]
-            hid_rows.append(jnp.concatenate([h, hid_lo[rows, :], h], axis=1))
-            left.append(dot(w_cols, jnp.concatenate([high, high, low, low], axis=0)))
+        for i in range(0, RED, 2):
+            pair = []
+            for j in (at * RED + i, at * RED + i + 1):
+                here = pl.ds(pl.multiple_of(j * C, C), C)
+                grad_raw = stage[here, :] * env_ref[here, :]
+                fraction = (position + (j * B).astype(F32)) * (1.0 / L)
+                decay_sum += grad_raw * raw_ref[here, :] * fraction
+                skip_sum += in_x[j].astype(F32) * in_g[j].astype(F32)
+                high, low = split(grad_raw)
+                right.append(jnp.concatenate([high, low], axis=0))
+                rows = pl.ds(pl.multiple_of(j * 64, 64), 64)
+                hid_rows.append(jnp.concatenate([hid_hi[rows, :], hid_lo[rows, :]], axis=0))
+                pair.append(jnp.concatenate([high, high, low, low], axis=0))
+            both = dot(w_cols, jnp.concatenate(pair, axis=1))
+            left += [both[:, :B], both[:, B:]]
         second += lax.dot_general(
             jnp.concatenate(hid_rows, axis=1),
             jnp.concatenate(right, axis=1),
@@ -353,7 +354,7 @@
         )
         rows = pl.ds(pl.multiple_of(at * RED * 64, RED * 64), RED * 64)
         high, low = split(jnp.concatenate(left, axis=0) * cos_ref[rows, :])
-        turned = dot(jnp.concatenate([high, low, high], axis=1), pt_ref[...])
+        turned = dot(jnp.concatenate([high, low], axis=1), pt_ref[...])
         for i in range(RED):
             j = at * RED + i
             part = turned[i * 64 : (i + 1) * 64]
@@ -366,17 +367,21 @@
         0,
         J // RED,
         reduce_filter,
-        (zero, zero, jnp.zeros((64, C), F32), jnp.zeros((64, B), F32), jnp.zeros((64, B), F32)),
+        (zero, zero, jnp.zeros((B, 2 * C), F32), jnp.zeros((64, B), F32), jnp.zeros((64, B), F32)),
     )
+    second = second[:64] + second[64:]
     wide[...] = jnp.zeros((B, B), F32)
-    wide[:64, :C] = second * scale
-    packed = jnp.transpose(wide[...])[:C]
+    wide[:64, : 2 * C] = second * scale
+    packed = jnp.transpose(wide[...])
+    packed = packed[:C] + packed[C : 2 * C]
     packed = jnp.where(lane[:8] < 64, packed[:8], pltpu.roll(packed[8:], 64, 1))
     row = lax.broadcasted_iota(jnp.int32, (C, B), 0)
     sums = jnp.where(lane == row, -scale * jnp.sum(decay_sum, axis=1, keepdims=True), 0.0)
     sums += jnp.where(lane == row + C, scale * jnp.sum(skip_sum, axis=1, keepdims=True), 0.0)
     sums = jnp.sum(sums, axis=0, keepdims=True)
 
+    cos_sum += pltpu.roll(cos_sum, B - 32, 1)
+    sin_sum += pltpu.roll(sin_sum, B - 32, 1)
     lane_64 = lax.broadcasted_iota(jnp.int32, (64, B), 1)
     swapped = jnp.where(lane_64 < 16, pltpu.roll(sin_sum, B - 16, 1), pltpu.roll(sin_sum, 16, 1))
     wide[:64, :] = (cos_sum + swapped) * scale
@@ -414,7 +419,9 @@
 
     spread(rs_in, my_z, rz_sem, 4, DEPTH, on_depth, rs_out)
     spread(z_in, my_z, z_sem, 5, DEPTH, on_depth)
-    exchange(back_g, grad_in, cg_sem, 3, 4, 32)
+    inverse(spec_h, spec_g, True)
+    finish(in_g, back_g)
+    exchange(back_g, grad_in, cg_sem, 3, 0, 32)
 
     def to_rows(in_ref, at, half):
         block = in_ref[pl.ds(at * 16, 16)].astype(F32)[:, half * 8 : (half + 1) * 8]
@@ -443,7 +450,7 @@
             gq_ref[:, lanes] = (go_ref[:, lanes].astype(F32) * to_rows(conv_in, at, half)).astype(BF16)
         return carry
 
-    lax.fori_loop(0, 4, rows_q, 0)
+    lax.fori_loop(0, 4, rows_q, 0, unroll=True)
 
     wait_bytes(tp_in, TP - 1, t_sem)
     fin[my_z] = add(tp_in, TP)
@@ -481,7 +488,7 @@
             gv_ref[:, lanes] = (k_ref[:, lanes].astype(F32) * grad).astype(BF16)
         return carry
 
-    lax.fori_loop(0, 4, rows_kv, 0)
+    lax.fori_loop(0, 4, rows_kv, 0, unroll=True)
 
     wait_bytes(fin, DEPTH - 1, f_sem)
     for i in range(DEPTH):

time: 76.9 us -> 75 us (0.975)
  Pallas kernels: 75.5 us -> 73.7 us
    pallas_call x1, Pallas kernels: 74.5 us -> 72.7 us  [per_device(): pl.pallas_call(kernel, out_shape=[pltpu.VMEM(x.shape, x.dtype) for x in s...]
where the time goes in v4:
time: 75 us; the launch traced here: 74.3 us
  Pallas kernels  73.7 us (98%)
    pallas_call x1, Pallas kernels, per_device(): pl.pallas_call(kernel, out_shape=[pltpu.VMEM(x.shape, x.dtype) for x in s...  72.7 us

profile of v4, /device:TPU:1, one launch (start us, length us, event | category | flops | bytes accessed | tf_op | source)
XLA Modules:
  0.0 74.3 jit_solution(9747443561614399722)
XLA Ops:
  0.6 72.7 %shard_map.207 = (bf16[128,1024]{1,0:T(8,128)(2,1)S(1)}, bf16[128,1024]{1,0:T(8,128)(2,1)S(1)}, bf16[128,1024]{1,0:T(8,128)(2,1)S(1)}, f32[32,64]{1,0:T(8,128)S(...) custom-call(bf16[128,1024]{1,0:T(8,128)(2,1)} %refs_0_.1, bf16[128,1024]{1,0:T(8,128)(2,1)} %refs_1_.1, ...), custom_call_target="tpu_custom_call" | custom-call | tf_op jit(solution)/shard_map/pallas_call | solution.py:541
  73.3 1.0 %shard_map.208 = (bf16[128,1024]{1,0:T(8,128)(2,1)}, bf16[128,1024]{1,0:T(8,128)(2,1)}, bf16[128,1024]{1,0:T(8,128)(2,1)}, f32[32,64]{1,0:T(8,128)}, f32[64,1024...) custom-call(bf16[128,1024]{1,0:T(8,128)(2,1)S(1)} %get-tuple-element.21.refs_0_, ...), custom_call_target="tpu_custom_call" | custom-call | tf_op jit(solution)/shard_map/pallas_call | solution.py:564

commit v5 on v4

--- a/solution.py
+++ b/solution.py
@@ -147,7 +147,7 @@
             out_ref[pl.ds(at * 16, 16)] = jnp.concatenate(parts, axis=1).astype(BF16)
             return carry
 
-        lax.fori_loop(0, 4, step, 0)
+        lax.fori_loop(0, 4, step, 0, unroll=True)
 
     def exchange(out_ref, in_ref, recv_sem, send_at, first, last):
         def send(peer):
@@ -370,16 +370,6 @@
         (zero, zero, jnp.zeros((B, 2 * C), F32), jnp.zeros((64, B), F32), jnp.zeros((64, B), F32)),
     )
     second = second[:64] + second[64:]
-    wide[...] = jnp.zeros((B, B), F32)
-    wide[:64, : 2 * C] = second * scale
-    packed = jnp.transpose(wide[...])
-    packed = packed[:C] + packed[C : 2 * C]
-    packed = jnp.where(lane[:8] < 64, packed[:8], pltpu.roll(packed[8:], 64, 1))
-    row = lax.broadcasted_iota(jnp.int32, (C, B), 0)
-    sums = jnp.where(lane == row, -scale * jnp.sum(decay_sum, axis=1, keepdims=True), 0.0)
-    sums += jnp.where(lane == row + C, scale * jnp.sum(skip_sum, axis=1, keepdims=True), 0.0)
-    sums = jnp.sum(sums, axis=0, keepdims=True)
-
     cos_sum += pltpu.roll(cos_sum, B - 32, 1)
     sin_sum += pltpu.roll(sin_sum, B - 32, 1)
     lane_64 = lax.broadcasted_iota(jnp.int32, (64, B), 1)
@@ -391,10 +381,6 @@
     for i in range(DEPTH):
         rs_out[i] = first[i : i + 1]
     rs_in[my_z] = rs_out[my_z]
-    wide[:8, :] = packed
-    wide[8:9, :] = sums
-    wide[9:16, :] = jnp.zeros((7, B), F32)
-    z_in[my_z] = wide[:C, :].astype(BF16)
 
     def spread(ref, mine, sem, send_at, count, peer_of, parts=None):
         def step(i, carry):
@@ -418,6 +404,19 @@
         return {"seq": peer * PLANE + my_y}
 
     spread(rs_in, my_z, rz_sem, 4, DEPTH, on_depth, rs_out)
+    wide[...] = jnp.zeros((B, B), F32)
+    wide[:64, : 2 * C] = second * scale
+    packed = jnp.transpose(wide[...])
+    packed = packed[:C] + packed[C : 2 * C]
+    packed = jnp.where(lane[:8] < 64, packed[:8], pltpu.roll(packed[8:], 64, 1))
+    row = lax.broadcasted_iota(jnp.int32, (C, B), 0)
+    sums = jnp.where(lane == row, -scale * jnp.sum(decay_sum, axis=1, keepdims=True), 0.0)
+    sums += jnp.where(lane == row + C, scale * jnp.sum(skip_sum, axis=1, keepdims=True), 0.0)
+    sums = jnp.sum(sums, axis=0, keepdims=True)
+    wide[:8, :] = packed
+    wide[8:9, :] = sums
+    wide[9:16, :] = jnp.zeros((7, B), F32)
+    z_in[my_z] = wide[:C, :].astype(BF16)
     spread(z_in, my_z, z_sem, 5, DEPTH, on_depth)
     inverse(spec_h, spec_g, True)
     finish(in_g, back_g)

time: 75 us -> 75.3 us (level)
  no operation moved by 1% of the time
where the time goes in v5:
time: 75.3 us; the launch traced here: 74.3 us
  Pallas kernels  73.6 us (98%)
    pallas_call x1, Pallas kernels, per_device(): pl.pallas_call(kernel, out_shape=[pltpu.VMEM(x.shape, x.dtype) for x in s...  72.6 us

profile of v5, /device:TPU:1, one launch (start us, length us, event | category | flops | bytes accessed | tf_op | source)
XLA Modules:
  0.0 74.3 jit_solution(5070699131076695719)
XLA Ops:
  0.6 72.6 %shard_map.207 = (bf16[128,1024]{1,0:T(8,128)(2,1)S(1)}, bf16[128,1024]{1,0:T(8,128)(2,1)S(1)}, bf16[128,1024]{1,0:T(8,128)(2,1)S(1)}, f32[32,64]{1,0:T(8,128)S(...) custom-call(bf16[128,1024]{1,0:T(8,128)(2,1)} %refs_0_.1, bf16[128,1024]{1,0:T(8,128)(2,1)} %refs_1_.1, ...), custom_call_target="tpu_custom_call" | custom-call | tf_op jit(solution)/shard_map/pallas_call | solution.py:540
  73.3 1.0 %shard_map.208 = (bf16[128,1024]{1,0:T(8,128)(2,1)}, bf16[128,1024]{1,0:T(8,128)(2,1)}, bf16[128,1024]{1,0:T(8,128)(2,1)}, f32[32,64]{1,0:T(8,128)}, f32[64,1024...) custom-call(bf16[128,1024]{1,0:T(8,128)(2,1)S(1)} %get-tuple-element.21.refs_0_, ...), custom_call_target="tpu_custom_call" | custom-call | tf_op jit(solution)/shard_map/pallas_call | solution.py:563
